TPU v7x, 32 devices: a whole 2x2x4 slice. The times are simulated.
32 devices in a mesh: cores: 8 (over y, x, core), face: 4 (over z).
Axes of the slice: x: 2, y: 2, z: 4, core: 2. Of those that a mesh axis runs over, the one named last changes fastest.
Arguments:
- fields: bfloat16 [2, 16, 16, 128, 256], P(None, 'cores', 'face'), may hold values from -6 to 6
- pore_mask: int32 [16, 16, 128], P('cores', 'face'), may hold values 0 or 1
- conv_kernel: bfloat16 [54, 32], replicated, may hold values from -0.875 to 0.875
- conv_bias: float32 [32], replicated, may hold values from -3 to 3
- read_weight: float32 [32], replicated, may hold values from -1 to 1
- obs_cells: int32 [2048], P(('cores', 'face')), may hold values from 0 to 1023
- obs_values: float32 [2048], P(('cores', 'face')), may hold values from 0 to 1
- obs_sigma: float32 [2048], P(('cores', 'face')), may hold values from 0.3 to 3
Outputs:
- analysis: bfloat16 [3, 16, 16, 128, 256], P(None, 'cores', 'face')
Inputs may be any that keep to these rules, and one draw needn't show every extreme that they name: obs_cells holds the index (z * 4 + x) * 128 + y of a cell in the block of the device that holds the observation.
All inputs are finite; a program needn't handle non-finite values. No bound on the sum of `pore_mask` on one device may be relied on, other than what follows from the above.
Results may differ from a plain program's by a relative error of at most 0.0091.
Values may be sent and summed in bfloat16 or wider, within the bound.
No kernel may reach another device: no remote copies, remote signals or barrier semaphores. Data moves between devices by JAX's collectives and lax.ppermute only.
A program may use at most 64 MiB of HBM per device.

v0:
```python
import functools
import math

import jax
import jax.numpy as jnp
import numpy as np
from jax import lax
from jax.experimental import pallas as pl
from jax.experimental.pallas import tpu as pltpu
from jax.sharding import PartitionSpec as P

HIGHEST = lax.Precision.HIGHEST
PAY_ROWS = 16
GATHER_DEVICES = 64
BLOCK = 64
SPANS = (16, 32, 32, 48)
VMEM_BYTES = 8 * 1024 * 1024


def plane_places(planes, columns):
    own = [(f, z + 1, x + 1) for f in range(2) for z in range(planes) for x in range(columns)]
    low = [(f, 0, x + 1) for f in range(2) for x in range(columns)]
    high = [(f, planes + 1, x + 1) for f in range(2) for x in range(columns)]
    left = [(f, z + 1, 0) for f in range(2) for z in range(planes)]
    right = [(f, z + 1, columns + 1) for f in range(2) for z in range(planes)]
    corners = [
        (f, z, x) for z in (0, planes + 1) for f in range(2) for x in (0, columns + 1)
    ]
    return own + low + high + left + right + corners


def tap_selector(planes, columns):
    places = plane_places(planes, columns)
    chosen = np.zeros((54, planes * columns, 3 * len(places)), np.float32)
    for z in range(planes):
        for x in range(columns):
            for n, (f, zz, xx) in enumerate(places):
                a, b = zz - z, xx - x
                if 0 <= a <= 2 and 0 <= b <= 2:
                    for c in range(3):
                        chosen[27 * f + 9 * a + 3 * b + c, z * columns + x, c * len(places) + n] = 1.0
    return chosen


def swap_matrix(outer, inner):
    matrix = np.zeros((outer * inner, outer * inner), np.float32)
    for i in range(outer):
        for j in range(inner):
            matrix[j * outer + i, i * inner + j] = 1.0
    return matrix


def three_pieces(value):
    first = lax.reduce_precision(value, 8, 7)
    second = lax.reduce_precision(value - first, 8, 7)
    third = lax.reduce_precision(value - first - second, 8, 7)
    return first, second, third


def ones_rows(members):
    row_index = lax.broadcasted_iota(jnp.int32, (16, members), 0)
    return jnp.where(row_index < 3, 1.0, 0.0).astype(jnp.bfloat16)


def observe_kernel(
    own, low, high, left, right, corner_low, corner_high, by_row, swap_in, read_column,
    observations, cells, mask, packed, pay_out, pred
):
    lanes, members = own.shape[1], own.shape[2]
    count = packed.shape[1]
    observed = cells.shape[0]
    packed[0] = jnp.zeros((count, members), jnp.bfloat16)
    packed[lanes + 1] = jnp.zeros((count, members), jnp.bfloat16)

    for step in range(lanes // 16):
        at = step * 16
        part = lambda ref: ref[:, pl.ds(at, 16), :]
        sides = (left, right, corner_low, corner_high)
        blocks = (
            part(own),
            jnp.concatenate([part(low), part(high)], axis=0),
            jnp.concatenate([part(side) for side in sides], axis=0),
        )
        for g, block in enumerate(blocks):
            moved = jnp.dot(
                swap_in[...], block.reshape(256, members), preferred_element_type=jnp.float32
            )
            packed[pl.ds(at + 1, 16), 16 * g : 16 * g + 16, :] = (
                moved.astype(jnp.bfloat16).reshape(16, 16, members)
            )

    ones = ones_rows(members)
    read = jnp.broadcast_to(read_column[...], (read_column.shape[0], members))

    def some_cells(step, carry):
        for k in range(16):
            o = step * 16 + k
            cell = cells[o]
            row, y = cell // lanes, cell % lanes
            taps = jnp.concatenate(
                [packed[pl.ds(y, 3)].reshape(3 * count, members), ones], axis=0
            )
            half = jnp.dot(by_row[row], taps, preferred_element_type=jnp.float32)
            total = jnp.sum(read * (half * (1.0 + jnp.tanh(half))), axis=0, keepdims=True)
            found = (0.5 + 0.5 * jnp.tanh(total)) * mask[row, y].astype(jnp.float32)
            pred[pl.ds(o, 1), :] = found.astype(jnp.bfloat16).astype(jnp.float32)
        return carry

    lax.fori_loop(0, observed // 16, some_cells, 0)

    root_count = math.sqrt(members - 1)
    predicted = pred[...]
    center = jnp.mean(predicted, axis=1, keepdims=True)
    inverse_sigma = 1.0 / observations[:, 0:1]
    scaled = (predicted - center) * (inverse_sigma / root_count)
    innovation = (observations[:, 1:2] - center) * inverse_sigma
    coeff = jnp.sum(scaled * innovation, axis=0, keepdims=True) / root_count
    first = coeff.astype(jnp.bfloat16).astype(jnp.float32)
    second = (coeff - first).astype(jnp.bfloat16).astype(jnp.float32)
    third = coeff - first - second
    index = lax.broadcasted_iota(jnp.int32, (PAY_ROWS, members), 0)
    tail = jnp.where(index == 0, first, jnp.where(index == 1, second, jnp.where(index == 2, third, 0.0)))
    pay_out[0:observed, :] = scaled.astype(jnp.bfloat16)
    pay_out[observed : observed + PAY_ROWS, :] = tail.astype(jnp.bfloat16)


def saturate_kernel(
    start, packed, weights, swap_out, mask, read_half, anomaly_out, mean_out, sat_rows
):
    rows, span, members = anomaly_out.shape
    count = packed.shape[1]
    channels = read_half.shape[0]
    ones = ones_rows(members)
    lane_index = lax.broadcasted_iota(jnp.int32, mask.shape, 1)

    def some_rows(step, carry):
        found = []
        for k in range(8):
            y = start + step * 8 + k
            taps = jnp.concatenate(
                [packed[pl.ds(y, 3)].reshape(3 * count, members), ones], axis=0
            )
            half = jnp.dot(weights[...], taps, preferred_element_type=jnp.float32)
            total = jnp.zeros((rows, members), jnp.float32)
            for c in range(channels):
                part = half[rows * c : rows * c + rows]
                total = total + read_half[c] * (part * (1.0 + jnp.tanh(part)))
            here = jnp.sum(jnp.where(lane_index == y, mask[...], 0.0), axis=1, keepdims=True)
            found.append(here * (0.5 + 0.5 * jnp.tanh(total)))
        at = pl.multiple_of(step * 8 * rows, 8 * rows)
        sat_rows[pl.ds(at, 8 * rows), :] = jnp.concatenate(found, axis=0).astype(jnp.bfloat16)
        return carry

    lax.fori_loop(0, span // 8, some_rows, 0)
    for n in range(span // 16):
        block = sat_rows[n * 16 * rows : (n + 1) * 16 * rows, :]
        moved = jnp.dot(swap_out[...], block, preferred_element_type=jnp.float32)
        mean = jnp.mean(moved, axis=1, keepdims=True)
        anomalies = (moved - mean).astype(jnp.bfloat16)
        anomaly_out[:, n * 16 : n * 16 + 16, :] = anomalies.reshape(rows, 16, members)
        mean_out[:, n * 16 : n * 16 + 16, :] = mean.reshape(rows, 16, 1)


def moments_kernel(fields, anomaly_out, mean_out):
    def step(n, carry):
        state = fields[pl.ds(2 * n, 2)].astype(jnp.float32)
        mean = jnp.mean(state, axis=2, keepdims=True)
        anomaly_out[pl.ds(2 * n, 2)] = (state - mean).astype(jnp.bfloat16)
        mean_out[pl.ds(2 * n, 2)] = mean
        return carry

    lax.fori_loop(0, fields.shape[0] // 2, step, 0)


def transposed_dot(a, b, precision):
    return lax.dot_general(
        a, b, (((0,), (0,)), ((), ())), preferred_element_type=jnp.float32, precision=precision
    )


def spread_row(part, p):
    return jnp.broadcast_to(part[p : p + 1, :], part.shape)


def spread_lane(part, q):
    return jnp.broadcast_to(part[:, q : q + 1], part.shape)


def inverse_factor_block(block):
    lane = lax.broadcasted_iota(jnp.int32, (8, 2 * BLOCK), 1)
    sub = lax.broadcasted_iota(jnp.int32, (8, 2 * BLOCK), 0)
    groups = BLOCK // 8
    parts = []
    for i in range(groups):
        unit = jnp.where(lane == sub + (BLOCK + 8 * i), 1.0, 0.0)
        known = jnp.concatenate(
            [block[8 * i : 8 * i + 8, :], jnp.zeros((8, BLOCK), jnp.float32)], axis=1
        )
        parts.append(known + unit)
    done = []
    upcoming = [spread_lane(parts[0], q) for q in range(8)]
    for j in range(groups):
        corner = upcoming
        entry = {(p, q): spread_row(corner[q], p) for q in range(8) for p in range(q, 8)}
        line = [spread_row(parts[j], p) for p in range(8)]
        near = j + 1 < groups
        if near:
            beside = [spread_lane(parts[j + 1], 8 * j + q) for q in range(8)]
            upcoming = [spread_lane(parts[j + 1], 8 * j + 8 + q) for q in range(8)]
        factor, scale = {}, []
        for q in range(8):
            root = lax.rsqrt(entry[q, q])
            scale.append(root)
            line[q] = line[q] * root
            for p in range(q + 1, 8):
                factor[p, q] = entry[p, q] * root
            for t in range(q + 1, 8):
                for p in range(t, 8):
                    entry[p, t] = entry[p, t] - factor[p, q] * factor[t, q]
            for p in range(q + 1, 8):
                line[p] = line[p] - factor[p, q] * line[q]
            if near:
                lead = beside[q] * root
                upcoming = [
                    column - lead * spread_row(lead, p) for p, column in enumerate(upcoming)
                ]
                for t in range(q + 1, 8):
                    beside[t] = beside[t] - lead * factor[t, q]
                parts[j + 1] = parts[j + 1] - lead * line[q]
        if j + 2 < groups:
            weighted = [None] * 8
            for q in range(7, -1, -1):
                rest = line[q]
                for p in range(q + 1, 8):
                    rest = rest - factor[p, q] * weighted[p]
                weighted[q] = rest * scale[q]
            for i in range(j + 2, groups):
                change = spread_lane(parts[i], 8 * j) * weighted[0]
                for q in range(1, 8):
                    change = change + spread_lane(parts[i], 8 * j + q) * weighted[q]
                parts[i] = parts[i] - change
        merged = line[0]
        for q in range(1, 8):
            merged = jnp.where(sub == q, line[q], merged)
        done.append(merged[:, BLOCK:])
    return jnp.concatenate(done, axis=0)


def update_kernel(gathered, *refs):
    if gathered:
        pay, refs = refs[0], refs[1:]
    else:
        gram, coeff_in, refs = refs[0], refs[1], refs[2:]
    moments, (out, joint, mixing) = refs[:-3], refs[-3:]
    members = out.shape[2]
    sub = lax.broadcasted_iota(jnp.int32, (members, members), 0)
    lane = lax.broadcasted_iota(jnp.int32, (members, members), 1)
    identity = jnp.where(sub == lane, 1.0, 0.0)
    if gathered:
        devices, observed = pay.shape[0], pay.shape[1] - PAY_ROWS
        group = max(1, 256 // observed)
        total = identity
        for d in range(0, devices, group):
            block = pay[d : d + group, 0:observed, :].reshape(-1, members)
            total = total + transposed_dot(block, block, None)
        coeff = jnp.zeros((PAY_ROWS, members), jnp.float32)
        for d in range(devices):
            coeff = coeff + pay[d, observed:, :].astype(jnp.float32)
        coeff = jnp.sum(coeff, axis=0, keepdims=True)
    else:
        total = identity + gram[...]
        coeff = coeff_in[...]
    joint[...] = total
    for k in range(members // BLOCK):
        at = k * BLOCK
        below = at + BLOCK
        wide_sub, wide_lane = sub[0:BLOCK, :], lane[0:BLOCK, :]
        inside = jnp.logical_and(wide_lane >= at, wide_lane < below)
        row = joint[at:below, :]
        inverse = inverse_factor_block(row[:, at:below])
        unit = jnp.where(wide_lane == wide_sub + at, 1.0, 0.0)
        row = jnp.dot(
            inverse,
            jnp.where(inside, unit, row),
            precision=HIGHEST,
            preferred_element_type=jnp.float32,
        )
        joint[at:below, :] = row
        if below < members:
            ahead = jnp.where(wide_lane >= below, row, 0.0)
            change = transposed_dot(ahead, row, HIGHEST)
            rest_lane = lane[below:, :]
            inside = jnp.logical_and(rest_lane >= at, rest_lane < below)
            joint[below:, :] = jnp.where(inside, 0.0, joint[below:, :]) - change[below:, :]
    inverse = jnp.where(lane <= sub, joint[...], 0.0)
    half = jnp.sum(inverse * coeff, axis=1, keepdims=True)
    weight = jnp.sum(inverse * half, axis=0, keepdims=True)
    mixing[...] = jnp.transpose((inverse + weight).astype(jnp.bfloat16))

    def blend(anomalies, mean):
        outer, inner = anomalies.shape[0], anomalies.shape[1]
        moved = jnp.dot(
            anomalies.reshape(outer * inner, members), mixing[...], preferred_element_type=jnp.float32
        )
        return (mean + moved.reshape(outer, inner, members)).astype(jnp.bfloat16)

    anomalies, mean = moments[:2]
    field_rows = anomalies.shape[0]

    def step(n, carry):
        for k in range(2):
            at = 4 * n + 2 * k
            out[pl.ds(at, 2)] = blend(anomalies[pl.ds(at, 2)], mean[pl.ds(at, 2)])
        return carry

    lax.fori_loop(0, field_rows // 4, step, 0)
    at = 0
    for n in range(1, len(moments) // 2):
        anomalies, mean = moments[2 * n : 2 * n + 2]
        span = anomalies.shape[1]
        out[field_rows:, at : at + span, :] = blend(anomalies[...], mean[...])
        at += span


def shift(value, axis, by, closed):
    count = lax.axis_size(axis)
    if by > 0:
        pairs = [(i, (i + 1) % count) for i in range(count if closed else count - 1)]
    else:
        pairs = [((i + 1) % count, i) for i in range(count if closed else count - 1)]
    return lax.ppermute(value, axis, pairs)


def gather_rows(block, steps, packed, saturate):
    pieces = []
    for n, (axis, bit) in enumerate(steps):
        count = lax.axis_size(axis)
        if n < len(SPANS):
            block, packed = lax.optimization_barrier((block, packed))
        other = lax.ppermute(block, axis, [(i, i ^ bit) for i in range(count)])
        if n < len(SPANS):
            piece = saturate(n, packed)
        block = jnp.concatenate([block, other], axis=0)
        if n < len(SPANS):
            block, piece = lax.optimization_barrier((block, piece))
            pieces.append(piece)
    return block, pieces + [saturate(n, packed) for n in range(len(pieces), len(SPANS))]


def bits_of(axis, count):
    bits = []
    while (1 << len(bits)) < count:
        bits.append((axis, 1 << len(bits)))
    return bits


def vmem():
    return pl.BlockSpec(memory_space=pltpu.VMEM)


def smem():
    return pl.BlockSpec(memory_space=pltpu.SMEM)


def moments_shape(outer, inner, members):
    return (
        jax.ShapeDtypeStruct((outer, inner, members), jnp.bfloat16),
        jax.ShapeDtypeStruct((outer, inner, 1), jnp.float32),
    )


def shards(
    fields, pore_mask, conv_kernel, conv_bias, read_weight, obs_cells, obs_values, obs_sigma
):
    _, planes, columns, lanes, members = fields.shape
    channels = conv_kernel.shape[1]
    rows = planes * columns
    observed = obs_cells.shape[0]

    left = shift(fields[:, :, -1:], "face", 1, False)
    right = shift(fields[:, :, :1], "face", -1, False)
    low = shift(fields[:, -1:], "cores", 1, True)
    high = shift(fields[:, :1], "cores", -1, True)
    low_sides = jnp.concatenate([left[:, -1:], right[:, -1:]], axis=2)
    high_sides = jnp.concatenate([left[:, :1], right[:, :1]], axis=2)
    corner_low = shift(low_sides, "cores", 1, True)
    corner_high = shift(high_sides, "cores", -1, True)

    selector = tap_selector(planes, columns)
    count = selector.shape[2] // 3
    taps = jnp.dot(
        jnp.transpose(conv_kernel),
        jnp.asarray(selector.reshape(54, -1), jnp.bfloat16),
        preferred_element_type=jnp.float32,
    ).reshape(channels, rows, 3 * count)
    bias = jnp.stack(three_pieces(0.5 * conv_bias), axis=1)
    bias = jnp.broadcast_to(bias[:, None, :], (channels, rows, 3))
    weights = jnp.concatenate(
        [0.5 * taps, bias, jnp.zeros((channels, rows, 13), jnp.float32)], axis=2
    ).astype(jnp.bfloat16)
    by_row = jnp.transpose(weights, (1, 0, 2))
    weights = weights.reshape(channels * rows, 3 * count + 16)
    flat = lambda a: a.reshape(-1, lanes, members)
    starts = [sum(SPANS[:n]) for n in range(len(SPANS))]
    mask = pore_mask.reshape(rows, lanes)
    mask_float = mask.astype(jnp.float32)
    read_half = 0.5 * read_weight
    swap_in = jnp.asarray(swap_matrix(16, 16), jnp.bfloat16)
    swap_out = jnp.asarray(swap_matrix(16, rows), jnp.bfloat16)
    params = pltpu.CompilerParams(vmem_limit_bytes=VMEM_BYTES)
    field_moments = pl.pallas_call(
        moments_kernel,
        out_shape=moments_shape(2 * rows, lanes, members),
        in_specs=[vmem()],
        out_specs=(vmem(), vmem()),
        compiler_params=params,
        name="moments",
    )(flat(fields))
    read_column = read_half[:, None]
    observations = jnp.stack([obs_sigma, obs_values], axis=1)
    packed, pay = pl.pallas_call(
        observe_kernel,
        out_shape=(
            jax.ShapeDtypeStruct((lanes + 2, count, members), jnp.bfloat16),
            jax.ShapeDtypeStruct((observed + PAY_ROWS, members), jnp.bfloat16),
        ),
        in_specs=[vmem()] * 11 + [smem()] * 2,
        out_specs=(vmem(), vmem()),
        scratch_shapes=[pltpu.VMEM((observed, members), jnp.float32)],
        compiler_params=params,
        name="observe",
    )(
        flat(fields), flat(low), flat(high), flat(left), flat(right), flat(corner_low),
        flat(corner_high), by_row, swap_in, read_column, observations, obs_cells, mask,
    )

    def saturate(n, packed):
        span = SPANS[n]
        return pl.pallas_call(
            functools.partial(saturate_kernel, starts[n]),
            out_shape=moments_shape(rows, span, members),
            in_specs=[vmem()] * 4 + [smem()],
            out_specs=(vmem(), vmem()),
            scratch_shapes=[pltpu.VMEM((rows * span, members), jnp.bfloat16)],
            compiler_params=params,
            cost_estimate=pl.CostEstimate(
                flops=2 * 256 * 256 * span * members,
                bytes_accessed=4 * 1024 * 1024,
                transcendentals=channels * rows * span * members,
            ),
            name="saturate",
        )(packed, weights, swap_out, mask_float, read_half)

    core_count, face_count = lax.axis_size("cores"), lax.axis_size("face")
    devices = core_count * face_count
    gathered = devices <= GATHER_DEVICES and devices & (devices - 1) == 0
    if gathered:
        steps = bits_of("face", face_count)[::-1] + bits_of("cores", core_count)[1:]
        steps = steps + bits_of("cores", core_count)[:1]
        block, pieces = gather_rows(pay[None], steps, packed, saturate)
        terms = (block,)
    else:
        part = pay[:observed]
        gram = lax.dot_general(
            part, part, (((0,), (0,)), ((), ())), preferred_element_type=jnp.float32
        )
        coeff = jnp.sum(pay[observed:].astype(jnp.float32), axis=0, keepdims=True)
        terms = lax.psum((gram, coeff), ("cores", "face"))
        pieces = [saturate(n, packed) for n in range(len(SPANS))]
    out = pl.pallas_call(
        functools.partial(update_kernel, gathered),
        out_shape=jax.ShapeDtypeStruct((3 * rows, lanes, members), jnp.bfloat16),
        in_specs=[vmem()] * (len(terms) + 2 + 2 * len(SPANS)),
        out_specs=vmem(),
        scratch_shapes=[
            pltpu.VMEM((members, members), jnp.float32),
            pltpu.VMEM((members, members), jnp.bfloat16),
        ],
        compiler_params=params,
        name="update",
    )(*terms, *field_moments, *(part for piece in pieces for part in piece))
    return out.reshape(3, planes, columns, lanes, members)


def solution(mesh):
    return jax.shard_map(
        shards,
        mesh=mesh,
        in_specs=(
            P(None, "cores", "face", None, None),
            P("cores", "face", None),
            P(),
            P(),
            P(),
            P(("cores", "face")),
            P(("cores", "face")),
            P(("cores", "face")),
        ),
        out_specs=P(None, "cores", "face", None, None),
        check_vma=False,
    )
```

profile of v0, /device:TPU:0, one launch (start us, length us, event | category | flops | bytes accessed | tf_op | source)
XLA Modules:
  0.0 70.6 jit_solution(9106278075801470092)
XLA Ops:
  0.0 1.9 %fusion.5 = (bf16[2,2,1,128,256]{4,3,2,1,0:T(8,128)(2,1)S(1)}, bf16[2,2,1,128,256]{4,3,2,1,0:T(8,128)(2,1)}) fusion(bf16[2,2,4,128,256]{4,3,2,1,0:T(8,128)(2,1)} %param.11), kind=kLoop, calls=%fused_computation.23 | loop fusion | bytes 1048576 | tf_op jit(solution)/shard_map/slice | solution.py:381
  1.9 1.4 %collective-permute-start.3 = (bf16[2,2,1,128,256]{4,3,2,1,0:T(8,128)(2,1)S(1)}, bf16[2,2,1,128,256]{4,3,2,1,0:T(8,128)(2,1)S(1)}, u32[]{:S(2)}, u32[]{:S(2)}) collective-permute-start(bf16[2,2,1,128,256]{4,3,2,1,0:T(8,128)(2,1)S(1)} %get-tuple-element.69), channel_id=1, source_target_pairs={{1,0},{2,1},{3,2},{5,4},{6,5},{7,6},{9,8},{10,9},{11,10},{13,12},{... | collective-permute-start | bytes 786440 | tf_op jit(solution)/shard_map/ppermute | solution.py:331
  3.3 5.6 %collective-permute-start.2 = (bf16[2,2,1,128,256]{4,3,2,1,0:T(8,128)(2,1)}, bf16[2,2,1,128,256]{4,3,2,1,0:T(8,128)(2,1)S(1)}, u32[]{:S(2)}, u32[]{:S(2)}) collective-permute-start(bf16[2,2,1,128,256]{4,3,2,1,0:T(8,128)(2,1)} %get-tuple-element.70), channel_id=1, source_target_pairs={{0,1},{1,2},{2,3},{4,5},{5,6},{6,7},{8,9},{9,10},{10,11},{12,13},{... | collective-permute-start | bytes 786440 | tf_op jit(solution)/shard_map/ppermute | solution.py:331
  8.9 1.1 %fusion.6 = (bf16[2,1,4,128,256]{4,3,2,1,0:T(8,128)(2,1)}, bf16[2,1,4,128,256]{4,3,2,1,0:T(8,128)(2,1)}) fusion(bf16[2,2,4,128,256]{4,3,2,1,0:T(8,128)(2,1)S(1)} %copy-done.1), kind=kLoop, calls=%fused_computation.24 | loop fusion | bytes 2097152 | tf_op jit(solution)/shard_map/slice | solution.py:383
  10.0 1.8 %collective-permute-start.1 = (bf16[2,1,4,128,256]{4,3,2,1,0:T(8,128)(2,1)}, bf16[2,1,4,128,256]{4,3,2,1,0:T(8,128)(2,1)S(1)}, u32[]{:S(2)}, u32[]{:S(2)}) collective-permute-start(bf16[2,1,4,128,256]{4,3,2,1,0:T(8,128)(2,1)} %get-tuple-element.71), channel_id=1, source_target_pairs={{4,0},{8,4},{12,8},{16,12},{20,16},{24,20},{28,24},{0,28},{5,1},{9... | collective-permute-start | bytes 1572872 | tf_op jit(solution)/shard_map/ppermute | solution.py:331
  11.8 0.1 copy.23
  11.9 0.1 fusion.1
  12.1 0.2 mul.24
  12.5 0.7 %collective-permute-done.3 = bf16[2,2,1,128,256]{4,3,2,1,0:T(8,128)(2,1)S(1)} collective-permute-done((bf16[2,2,1,128,256]{4,3,2,1,0:T(8,128)(2,1)S(1)}, bf16[2,2,1,128,256]{4,3,2,1,0:T(8,128)(2,1)S(1)}, u32[]{:S(2)}, u32[]{:S(2)}) %collective-permute-start.3) | collective-permute-done | bytes 262176 | tf_op jit(solution)/shard_map/ppermute | solution.py:331
  13.3 1.5 %collective-permute-done.2 = bf16[2,2,1,128,256]{4,3,2,1,0:T(8,128)(2,1)S(1)} collective-permute-done((bf16[2,2,1,128,256]{4,3,2,1,0:T(8,128)(2,1)}, bf16[2,2,1,128,256]{4,3,2,1,0:T(8,128)(2,1)S(1)}, u32[]{:S(2)}, u32[]{:S(2)}) %collective-permute-start.2) | collective-permute-done | bytes 262176 | tf_op jit(solution)/shard_map/ppermute | solution.py:331
  14.8 0.7 %pad_maximum_fusion.3 = bf16[2,1,2,128,256]{4,3,2,1,0:T(8,128)(2,1)} fusion(bf16[2,1,1,128,256]{4,3,2,1,0:T(8,128)(2,1)S(1)} %get-tuple-element.76, bf16[2,1,1,128,256]{4,3,2,1,0:T(8,128)(2,1)S(1)} %get-tuple-element.74), kind=kLoop, calls=%fused_computation.6 | loop fusion | flops 131072 | bytes 524288 | tf_op jit(solution)/shard_map/concatenate | solution.py:384
  15.5 0.7 %pad_maximum_fusion.4 = bf16[2,1,2,128,256]{4,3,2,1,0:T(8,128)(2,1)} fusion(bf16[2,1,1,128,256]{4,3,2,1,0:T(8,128)(2,1)S(1)} %get-tuple-element.75, bf16[2,1,1,128,256]{4,3,2,1,0:T(8,128)(2,1)S(1)} %get-tuple-element.73), kind=kLoop, calls=%fused_computation.7 | loop fusion | flops 131072 | bytes 524288 | tf_op jit(solution)/shard_map/concatenate | solution.py:385
  16.3 2.6 %collective-permute-start.5 = (bf16[2,1,2,128,256]{4,3,2,1,0:T(8,128)(2,1)}, bf16[2,1,2,128,256]{4,3,2,1,0:T(8,128)(2,1)S(1)}, u32[]{:S(2)}, u32[]{:S(2)}) collective-permute-start(bf16[2,1,2,128,256]{4,3,2,1,0:T(8,128)(2,1)} %pad_maximum_fusion.4), channel_id=1, source_target_pairs={{4,0},{8,4},{12,8},{16,12},{20,16},{24,20},{28,24},{0,28},{5,1},{9... | collective-permute-start | bytes 786440 | tf_op jit(solution)/shard_map/ppermute | solution.py:331
  18.9 0.9 %mul.21 = bf16[32,8,144]{2,1,0:T(8,128)(2,1)} reshape(bf16[32,1152]{1,0:T(8,128)(2,1)S(1)} %fusion.1) | data formatting | bytes 147456 | tf_op jit(solution)/shard_map/mul | solution.py:399
  20.0 0.9 %copy.24 = bf16[32,8,144]{2,0,1:T(8,128)(2,1)S(1)} copy(bf16[32,8,144]{2,1,0:T(8,128)(2,1)} %mul.21) | data formatting | bytes 147456 | tf_op jit(solution)/shard_map/mul | solution.py:399
  21.0 10.4 %collective-permute-done.4 = bf16[2,1,2,128,256]{4,3,2,1,0:T(8,128)(2,1)S(1)} collective-permute-done((bf16[2,1,2,128,256]{4,3,2,1,0:T(8,128)(2,1)}, bf16[2,1,2,128,256]{4,3,2,1,0:T(8,128)(2,1)S(1)}, u32[]{:S(2)}, u32[]{:S(2)}) %collective-permute-start.4) | collective-permute-done | bytes 262176 | tf_op jit(solution)/shard_map/ppermute | solution.py:331
  31.5 3.2 %observe.1 = (bf16[130,48,256]{2,1,0:T(8,128)(2,1)S(1)}, bf16[80,256]{1,0:T(8,128)(2,1)S(1)}) custom-call(bf16[16,128,256]{2,1,0:T(8,128)(2,1)S(1)} %bitcast.28, bf16[8,128,256]{2,1,0:T(8,128)(2,1)S(1)} %bitcast.33, bf16[8,128,256]{2,1,0:T(8,128)(2,1)S(1)} %bitcast.32, bf16[4,128,256]{2,1,0:T(8,128)(2,1)S(1)} %bitcast.31, bf16[4,128,256]{2,1,0:T(8,128)(2,1)S(1)} %bitcast.30, ...), custom_call_target="tpu_custom_call" | custom-call | tf_op jit(solution)/shard_map/observe/pallas_call | solution.py:421
  34.7 2.7 %collective-permute-start.6 = (bf16[1,80,256]{2,1,0:T(8,128)(2,1)S(1)}, bf16[1,80,256]{2,1,0:T(8,128)(2,1)S(1)}, u32[]{:S(2)}, u32[]{:S(2)}) collective-permute-start(bf16[1,80,256]{2,1,0:T(8,128)(2,1)S(1)} %bitcast.36), channel_id=1, source_target_pairs={{0,2},{1,3},{2,0},{3,1},{4,6},{5,7},{6,4},{7,5},{8,10},{9,11},{10,... | collective-permute-start | bytes 122888 | tf_op jit(solution)/shard_map/ppermute | solution.py:340
  37.4 2.0 %saturate.4 = (bf16[8,16,256]{2,1,0:T(8,128)(2,1)S(1)}, f32[8,16,1]{2,1,0:T(8,128)S(1)}) custom-call(bf16[130,48,256]{2,1,0:T(8,128)(2,1)S(1)} %get-tuple-element.55.packed, bf16[256,160]{1,0:T(8,128)(2,1)S(1)} %maximum_maximum_fusion.weights, bf16[128,128]{1,0:T(8,128)(2,1)S(1)} %copy-done.3, f32[8,128]{1,0:T(8,128)S(1)} %convert_element_type.5.mask, ...), custom_call_target="tpu_custom_call" | custom-call | flops 536870912 | bytes 4194304 | tf_op jit(solution)/shard_map/saturate/pallas_call | solution.py:439
  39.4 0.3 collective-permute-done.6
  39.7 1.6 %collective-permute-start.7 = (bf16[2,80,256]{2,1,0:T(8,128)(2,1)S(1)}, bf16[2,80,256]{2,1,0:T(8,128)(2,1)S(1)}, u32[]{:S(2)}, u32[]{:S(2)}) collective-permute-start(bf16[2,80,256]{2,1,0:T(8,128)(2,1)S(1)} %pad_maximum_fusion.6), channel_id=1, source_target_pairs={{0,1},{1,0},{2,3},{3,2},{4,5},{5,4},{6,7},{7,6},{8,9},{9,8},{10,11... | collective-permute-start | bytes 245768 | tf_op jit(solution)/shard_map/ppermute | solution.py:340
  41.3 3.3 %saturate.5 = (bf16[8,32,256]{2,1,0:T(8,128)(2,1)S(1)}, f32[8,32,1]{2,1,0:T(8,128)S(1)}) custom-call(bf16[130,48,256]{2,1,0:T(8,128)(2,1)S(1)} %get-tuple-element.55.packed, bf16[256,160]{1,0:T(8,128)(2,1)S(1)} %maximum_maximum_fusion.weights, bf16[128,128]{1,0:T(8,128)(2,1)S(1)} %copy-done.3, f32[8,128]{1,0:T(8,128)S(1)} %convert_element_type.5.mask, ...), custom_call_target="tpu_custom_call" | custom-call | flops 1073741824 | bytes 4194304 | tf_op jit(solution)/shard_map/saturate/pallas_call | solution.py:439
  44.6 0.2 collective-permute-start.8
  44.9 3.3 %saturate.6 = (bf16[8,32,256]{2,1,0:T(8,128)(2,1)S(1)}, f32[8,32,1]{2,1,0:T(8,128)S(1)}) custom-call(bf16[130,48,256]{2,1,0:T(8,128)(2,1)S(1)} %get-tuple-element.55.packed, bf16[256,160]{1,0:T(8,128)(2,1)S(1)} %maximum_maximum_fusion.weights, bf16[128,128]{1,0:T(8,128)(2,1)S(1)} %copy-done.3, f32[8,128]{1,0:T(8,128)S(1)} %convert_element_type.5.mask, ...), custom_call_target="tpu_custom_call" | custom-call | flops 1073741824 | bytes 4194304 | tf_op jit(solution)/shard_map/saturate/pallas_call | solution.py:439
  48.2 1.9 %collective-permute-done.8 = bf16[4,80,256]{2,1,0:T(8,128)(2,1)S(1)} collective-permute-done((bf16[4,80,256]{2,1,0:T(8,128)(2,1)S(1)}, bf16[4,80,256]{2,1,0:T(8,128)(2,1)S(1)}, u32[]{:S(2)}, u32[]{:S(2)}) %collective-permute-start.8) | collective-permute-done | bytes 163872 | tf_op jit(solution)/shard_map/ppermute | solution.py:340
  50.1 0.6 collective-permute-start.9
  50.6 4.5 %saturate.7 = (bf16[8,48,256]{2,1,0:T(8,128)(2,1)S(1)}, f32[8,48,1]{2,1,0:T(8,128)S(1)}) custom-call(bf16[130,48,256]{2,1,0:T(8,128)(2,1)S(1)} %get-tuple-element.55.packed, bf16[256,160]{1,0:T(8,128)(2,1)S(1)} %maximum_maximum_fusion.weights, bf16[128,128]{1,0:T(8,128)(2,1)S(1)} %copy-done.3, f32[8,128]{1,0:T(8,128)S(1)} %convert_element_type.5.mask, ...), custom_call_target="tpu_custom_call" | custom-call | flops 1610612736 | bytes 4194304 | tf_op jit(solution)/shard_map/saturate/pallas_call | solution.py:439
  55.2 2.0 %collective-permute-done.9 = bf16[8,80,256]{2,1,0:T(8,128)(2,1)S(1)} collective-permute-done((bf16[8,80,256]{2,1,0:T(8,128)(2,1)S(1)}, bf16[8,80,256]{2,1,0:T(8,128)(2,1)S(1)}, u32[]{:S(2)}, u32[]{:S(2)}) %collective-permute-start.9) | collective-permute-done | bytes 327712 | tf_op jit(solution)/shard_map/ppermute | solution.py:340
  57.3 0.9 %moments.1 = (bf16[16,128,256]{2,1,0:T(8,128)(2,1)S(1)}, f32[16,128,1]{2,1,0:T(8,128)S(1)}) custom-call(bf16[16,128,256]{2,1,0:T(8,128)(2,1)S(1)} %bitcast.29), custom_call_target="tpu_custom_call" | custom-call | tf_op jit(solution)/shard_map/moments/pallas_call | solution.py:411
  58.3 1.2 %collective-permute-done.10 = bf16[16,80,256]{2,1,0:T(8,128)(2,1)S(1)} collective-permute-done((bf16[16,80,256]{2,1,0:T(8,128)(2,1)S(1)}, bf16[16,80,256]{2,1,0:T(8,128)(2,1)S(1)}, u32[]{:S(2)}, u32[]{:S(2)}) %collective-permute-start.10) | collective-permute-done | bytes 655392 | tf_op jit(solution)/shard_map/ppermute | solution.py:340
  59.4 0.1 pad_maximum_fusion.refs_0_
  59.5 11.0 %update.1 = bf16[24,128,256]{2,1,0:T(8,128)(2,1)} custom-call(bf16[32,80,256]{2,1,0:T(8,128)(2,1)S(1)} %pad_maximum_fusion.refs_0_, bf16[16,128,256]{2,1,0:T(8,128)(2,1)S(1)} %get-tuple-element.59.refs_1_, f32[16,128,1]{2,1,0:T(8,128)S(1)} %get-tuple-element.60.refs_2_, bf16[8,16,256]{2,1,0:T(8,128)(2,1)S(1)} %get-tuple-element.61.refs_3_, ...), custom_call_target="tpu_custom_call" | custom-call | tf_op jit(solution)/shard_map/update/pallas_call | solution.py:470
  (48 shorter events, 0.8 us)
Async XLA Ops:
  0.0 11.9 %copy-start = (bf16[54,32]{0,1:T(8,128)(2,1)S(1)}, bf16[54,32]{0,1:T(8,128)(2,1)}, u32[]{:S(2)}) copy-start(bf16[54,32]{0,1:T(8,128)(2,1)} %param.13) | copy-start | bytes 10372
  0.0 8.9 %copy-start.1 = (bf16[2,2,4,128,256]{4,3,2,1,0:T(8,128)(2,1)S(1)}, bf16[2,2,4,128,256]{4,3,2,1,0:T(8,128)(2,1)}, u32[]{:S(2)}) copy-start(bf16[2,2,4,128,256]{4,3,2,1,0:T(8,128)(2,1)} %param.11) | copy-start | bytes 3145732
  1.9 9.9 %copy-start.7 = (f32[32]{0:T(128)S(1)}, f32[32]{0:T(128)}, u32[]{:S(2)}) copy-start(f32[32]{0:T(128)} %param.14) | copy-start | bytes 388
  1.9 10.0 %copy-start.6 = (bf16[54,1152]{1,0:T(8,128)(2,1)S(1)}, bf16[54,1152]{1,0:T(8,128)(2,1)}, u32[]{:S(2)}) copy-start(bf16[54,1152]{1,0:T(8,128)(2,1)} %constant.12.clone) | copy-start | bytes 373252
  1.9 11.3 %collective-permute-start.3 = (bf16[2,2,1,128,256]{4,3,2,1,0:T(8,128)(2,1)S(1)}, bf16[2,2,1,128,256]{4,3,2,1,0:T(8,128)(2,1)S(1)}, u32[]{:S(2)}, u32[]{:S(2)}) collective-permute-start(bf16[2,2,1,128,256]{4,3,2,1,0:T(8,128)(2,1)S(1)} %get-tuple-element.69), channel_id=1, source_target_pairs={{1,0},{2,1},{3,2},{5,4},{6,5},{7,6},{9,8},{10,9},{11,10},{13,12},{... | collective-permute-start | bytes 786440 | tf_op jit(solution)/shard_map/ppermute | solution.py:331
  3.3 9.2 %copy-start.10 = (f32[32]{0:T(128)S(1)}, f32[32]{0:T(128)}, u32[]{:S(2)}) copy-start(f32[32]{0:T(128)} %param.15) | copy-start | bytes 388
  3.3 11.4 %collective-permute-start.2 = (bf16[2,2,1,128,256]{4,3,2,1,0:T(8,128)(2,1)}, bf16[2,2,1,128,256]{4,3,2,1,0:T(8,128)(2,1)S(1)}, u32[]{:S(2)}, u32[]{:S(2)}) collective-permute-start(bf16[2,2,1,128,256]{4,3,2,1,0:T(8,128)(2,1)} %get-tuple-element.70), channel_id=1, source_target_pairs={{0,1},{1,2},{2,3},{4,5},{5,6},{6,7},{8,9},{9,10},{10,11},{12,13},{... | collective-permute-start | bytes 786440 | tf_op jit(solution)/shard_map/ppermute | solution.py:331
  10.0 21.5 %collective-permute-start.1 = (bf16[2,1,4,128,256]{4,3,2,1,0:T(8,128)(2,1)}, bf16[2,1,4,128,256]{4,3,2,1,0:T(8,128)(2,1)S(1)}, u32[]{:S(2)}, u32[]{:S(2)}) collective-permute-start(bf16[2,1,4,128,256]{4,3,2,1,0:T(8,128)(2,1)} %get-tuple-element.71), channel_id=1, source_target_pairs={{4,0},{8,4},{12,8},{16,12},{20,16},{24,20},{28,24},{0,28},{5,1},{9... | collective-permute-start | bytes 1572872 | tf_op jit(solution)/shard_map/ppermute | solution.py:331
  11.7 19.7 %collective-permute-start = (bf16[2,1,4,128,256]{4,3,2,1,0:T(8,128)(2,1)}, bf16[2,1,4,128,256]{4,3,2,1,0:T(8,128)(2,1)S(1)}, u32[]{:S(2)}, u32[]{:S(2)}) collective-permute-start(bf16[2,1,4,128,256]{4,3,2,1,0:T(8,128)(2,1)} %get-tuple-element.72), channel_id=1, source_target_pairs={{0,4},{4,8},{8,12},{12,16},{16,20},{20,24},{24,28},{28,0},{1,5},{5... | collective-permute-start | bytes 1572872 | tf_op jit(solution)/shard_map/ppermute | solution.py:331
  12.0 6.9 %copy-start.8 = (f32[64]{0:T(128)S(1)}, f32[64]{0:T(128)}, u32[]{:S(2)}) copy-start(f32[64]{0:T(128)} %param.17) | copy-start | bytes 772
  12.1 6.8 %copy-start.9 = (f32[64]{0:T(128)S(1)}, f32[64]{0:T(128)}, u32[]{:S(2)}) copy-start(f32[64]{0:T(128)} %param.18) | copy-start | bytes 772
  12.4 7.4 %copy-start.4 = (s32[2,4,128]{2,1,0:T(4,128)S(1)}, s32[2,4,128]{2,1,0:T(4,128)}, u32[]{:S(2)}) copy-start(s32[2,4,128]{2,1,0:T(4,128)} %param.12) | copy-start | bytes 12292
  13.3 18.2 %copy-start.2 = (bf16[256,256]{1,0:T(8,128)(2,1)S(1)}, bf16[256,256]{1,0:T(8,128)(2,1)}, u32[]{:S(2)}) copy-start(bf16[256,256]{1,0:T(8,128)(2,1)} %constant.13.clone.swap_in) | copy-start | bytes 393220
  13.3 18.2 %copy-start.5 = (s32[64]{0:T(128)S(1)}, s32[64]{0:T(128)}, u32[]{:S(2)}) copy-start(s32[64]{0:T(128)} %cells.1) | copy-start | bytes 772
  15.5 15.9 %collective-permute-start.4 = (bf16[2,1,2,128,256]{4,3,2,1,0:T(8,128)(2,1)}, bf16[2,1,2,128,256]{4,3,2,1,0:T(8,128)(2,1)S(1)}, u32[]{:S(2)}, u32[]{:S(2)}) collective-permute-start(bf16[2,1,2,128,256]{4,3,2,1,0:T(8,128)(2,1)} %pad_maximum_fusion.3), channel_id=1, source_target_pairs={{0,4},{4,8},{8,12},{12,16},{16,20},{20,24},{24,28},{28,0},{1,5},{5... | collective-permute-start | bytes 786440 | tf_op jit(solution)/shard_map/ppermute | solution.py:331
  16.3 15.2 %collective-permute-start.5 = (bf16[2,1,2,128,256]{4,3,2,1,0:T(8,128)(2,1)}, bf16[2,1,2,128,256]{4,3,2,1,0:T(8,128)(2,1)S(1)}, u32[]{:S(2)}, u32[]{:S(2)}) collective-permute-start(bf16[2,1,2,128,256]{4,3,2,1,0:T(8,128)(2,1)} %pad_maximum_fusion.4), channel_id=1, source_target_pairs={{4,0},{8,4},{12,8},{16,12},{20,16},{24,20},{28,24},{0,28},{5,1},{9... | collective-permute-start | bytes 786440 | tf_op jit(solution)/shard_map/ppermute | solution.py:331
  31.5 5.9 %copy-start.3 = (bf16[128,128]{1,0:T(8,128)(2,1)S(1)}, bf16[128,128]{1,0:T(8,128)(2,1)}, u32[]{:S(2)}) copy-start(bf16[128,128]{1,0:T(8,128)(2,1)} %constant.14.clone.swap_out) | copy-start | bytes 98308
  34.7 5.0 %collective-permute-start.6 = (bf16[1,80,256]{2,1,0:T(8,128)(2,1)S(1)}, bf16[1,80,256]{2,1,0:T(8,128)(2,1)S(1)}, u32[]{:S(2)}, u32[]{:S(2)}) collective-permute-start(bf16[1,80,256]{2,1,0:T(8,128)(2,1)S(1)} %bitcast.36), channel_id=1, source_target_pairs={{0,2},{1,3},{2,0},{3,1},{4,6},{5,7},{6,4},{7,5},{8,10},{9,11},{10,... | collective-permute-start | bytes 122888 | tf_op jit(solution)/shard_map/ppermute | solution.py:340
  39.7 4.9 %collective-permute-start.7 = (bf16[2,80,256]{2,1,0:T(8,128)(2,1)S(1)}, bf16[2,80,256]{2,1,0:T(8,128)(2,1)S(1)}, u32[]{:S(2)}, u32[]{:S(2)}) collective-permute-start(bf16[2,80,256]{2,1,0:T(8,128)(2,1)S(1)} %pad_maximum_fusion.6), channel_id=1, source_target_pairs={{0,1},{1,0},{2,3},{3,2},{4,5},{5,4},{6,7},{7,6},{8,9},{9,8},{10,11... | collective-permute-start | bytes 245768 | tf_op jit(solution)/shard_map/ppermute | solution.py:340
  44.6 5.4 %collective-permute-start.8 = (bf16[4,80,256]{2,1,0:T(8,128)(2,1)S(1)}, bf16[4,80,256]{2,1,0:T(8,128)(2,1)S(1)}, u32[]{:S(2)}, u32[]{:S(2)}) collective-permute-start(bf16[4,80,256]{2,1,0:T(8,128)(2,1)S(1)} %pad_maximum_fusion.5), channel_id=1, source_target_pairs={{0,8},{4,12},{8,0},{12,4},{16,24},{20,28},{24,16},{28,20},{1,9},{5... | collective-permute-start | bytes 491528 | tf_op jit(solution)/shard_map/ppermute | solution.py:340
  50.1 7.1 %collective-permute-start.9 = (bf16[8,80,256]{2,1,0:T(8,128)(2,1)S(1)}, bf16[8,80,256]{2,1,0:T(8,128)(2,1)S(1)}, u32[]{:S(2)}, u32[]{:S(2)}) collective-permute-start(bf16[8,80,256]{2,1,0:T(8,128)(2,1)S(1)} %pad_maximum_fusion.2), channel_id=1, source_target_pairs={{0,16},{4,20},{8,24},{12,28},{16,0},{20,4},{24,8},{28,12},{1,17},{... | collective-permute-start | bytes 983048 | tf_op jit(solution)/shard_map/ppermute | solution.py:340
  57.3 2.2 %collective-permute-start.10 = (bf16[16,80,256]{2,1,0:T(8,128)(2,1)S(1)}, bf16[16,80,256]{2,1,0:T(8,128)(2,1)S(1)}, u32[]{:S(2)}, u32[]{:S(2)}) collective-permute-start(bf16[16,80,256]{2,1,0:T(8,128)(2,1)S(1)} %pad_maximum_fusion.1), channel_id=1, source_target_pairs={{0,4},{4,0},{8,12},{12,8},{16,20},{20,16},{24,28},{28,24},{1,5},{5... | collective-permute-start | bytes 1966088 | tf_op jit(solution)/shard_map/ppermute | solution.py:340
where the time goes:
time: 70.8 us; the launch traced here: 70.6 us
  Pallas kernels  28.2 us (40%)
  waiting for transfers between devices  18 us (25%)
  starting transfers between devices  16.6 us (23%)
  local copies, waits for them, and re-layouts  5.4 us (8%)
  other arithmetic  1.94 us (3%)
    pallas_call x4, Pallas kernels, saturate(): pl.pallas_call(functools.partial(saturate_kernel, starts[n]), out_shape=m...  13.1 us
    ppermute x6, waiting for transfers between devices, shift(): return lax.ppermute(value, axis, pairs)  12.7 us
    ppermute x6, starting transfers between devices, shift(): return lax.ppermute(value, axis, pairs)  11.4 us
    pallas_call x1, Pallas kernels, shards(): pl.pallas_call(functools.partial(update_kernel, gathered), out_shape=jax....  11 us
    ppermute x5, waiting for transfers between devices, gather_rows(): other = lax.ppermute(block, axis, [(i, i ^ bit) for i in range(count)])  5.35 us
    ppermute x5, starting transfers between devices, gather_rows(): other = lax.ppermute(block, axis, [(i, i ^ bit) for i in range(count)])  5.19 us
    pallas_call x1, Pallas kernels, shards(): pl.pallas_call(observe_kernel, out_shape=(jax.ShapeDtypeStruct((lanes + 2...  3.21 us
    mul x3, local copies, waits for them, and re-layouts, shards(): 0.5 * taps  1.99 us
  transfers between devices with their start and end apart: 11, of which 7 were waited for; matrix products, arithmetic and copies ran while one was open for 8% of the time, Pallas kernels for 20%

commit v1 on v0

--- a/solution.py
+++ b/solution.py
@@ -12,8 +12,8 @@
 HIGHEST = lax.Precision.HIGHEST
 PAY_ROWS = 16
 GATHER_DEVICES = 64
-BLOCK = 64
-SPANS = (16, 32, 32, 48)
+BLOCK = 128
+SPANS = (16, 16, 48, 48)
 VMEM_BYTES = 8 * 1024 * 1024
 
 

time: 70.8 us -> 69.5 us (0.982)
  Pallas kernels: 28.2 us -> 27.3 us
  waiting for transfers between devices: 18 us -> 17.1 us
    pallas_call x1, Pallas kernels: 11 us -> 9.96 us  [shards(): pl.pallas_call(functools.partial(update_kernel, gathered), out_shape=jax....]
    ppermute x5, waiting for transfers between devices: 5.35 us -> 4.45 us  [gather_rows(): other = lax.ppermute(block, axis, [(i, i ^ bit) for i in range(count)])]
  transfers between devices with their start and end apart: 11 -> 11, of which waited for: 7 -> 8; matrix products, arithmetic and copies ran while one was open for 8% -> 8% of each run, Pallas kernels for 20% -> 20%
where the time goes in v1:
time: 69.5 us; the launch traced here: 69.3 us
  Pallas kernels  27.3 us (39%)
  starting transfers between devices  17.1 us (25%)
  waiting for transfers between devices  17.1 us (25%)
  local copies, waits for them, and re-layouts  5.4 us (8%)
  other arithmetic  1.94 us (3%)
    pallas_call x4, Pallas kernels, saturate(): pl.pallas_call(functools.partial(saturate_kernel, starts[n]), out_shape=m...  13.1 us
    ppermute x6, waiting for transfers between devices, shift(): return lax.ppermute(value, axis, pairs)  12.7 us
    ppermute x6, starting transfers between devices, shift(): return lax.ppermute(value, axis, pairs)  11.4 us
    pallas_call x1, Pallas kernels, shards(): pl.pallas_call(functools.partial(update_kernel, gathered), out_shape=jax....  9.96 us
    ppermute x5, starting transfers between devices, gather_rows(): other = lax.ppermute(block, axis, [(i, i ^ bit) for i in range(count)])  5.68 us
    ppermute x5, waiting for transfers between devices, gather_rows(): other = lax.ppermute(block, axis, [(i, i ^ bit) for i in range(count)])  4.45 us
    pallas_call x1, Pallas kernels, shards(): pl.pallas_call(observe_kernel, out_shape=(jax.ShapeDtypeStruct((lanes + 2...  3.4 us
    mul x3, local copies, waits for them, and re-layouts, shards(): 0.5 * taps  1.99 us
  transfers between devices with their start and end apart: 11, of which 8 were waited for; matrix products, arithmetic and copies ran while one was open for 8% of the time, Pallas kernels for 20%

profile of v1, /device:TPU:0, one launch (start us, length us, event | category | flops | bytes accessed | tf_op | source)
XLA Modules:
  0.0 69.3 jit_solution(3772390393022792596)
XLA Ops:
  0.0 1.9 %fusion.5 = (bf16[2,2,1,128,256]{4,3,2,1,0:T(8,128)(2,1)S(1)}, bf16[2,2,1,128,256]{4,3,2,1,0:T(8,128)(2,1)}) fusion(bf16[2,2,4,128,256]{4,3,2,1,0:T(8,128)(2,1)} %param.11), kind=kLoop, calls=%fused_computation.23 | loop fusion | bytes 1048576 | tf_op jit(solution)/shard_map/slice | solution.py:381
  1.9 1.4 %collective-permute-start.3 = (bf16[2,2,1,128,256]{4,3,2,1,0:T(8,128)(2,1)S(1)}, bf16[2,2,1,128,256]{4,3,2,1,0:T(8,128)(2,1)S(1)}, u32[]{:S(2)}, u32[]{:S(2)}) collective-permute-start(bf16[2,2,1,128,256]{4,3,2,1,0:T(8,128)(2,1)S(1)} %get-tuple-element.69), channel_id=1, source_target_pairs={{1,0},{2,1},{3,2},{5,4},{6,5},{7,6},{9,8},{10,9},{11,10},{13,12},{... | collective-permute-start | bytes 786440 | tf_op jit(solution)/shard_map/ppermute | solution.py:331
  3.3 5.6 %collective-permute-start.2 = (bf16[2,2,1,128,256]{4,3,2,1,0:T(8,128)(2,1)}, bf16[2,2,1,128,256]{4,3,2,1,0:T(8,128)(2,1)S(1)}, u32[]{:S(2)}, u32[]{:S(2)}) collective-permute-start(bf16[2,2,1,128,256]{4,3,2,1,0:T(8,128)(2,1)} %get-tuple-element.70), channel_id=1, source_target_pairs={{0,1},{1,2},{2,3},{4,5},{5,6},{6,7},{8,9},{9,10},{10,11},{12,13},{... | collective-permute-start | bytes 786440 | tf_op jit(solution)/shard_map/ppermute | solution.py:331
  8.9 1.1 %fusion.6 = (bf16[2,1,4,128,256]{4,3,2,1,0:T(8,128)(2,1)}, bf16[2,1,4,128,256]{4,3,2,1,0:T(8,128)(2,1)}) fusion(bf16[2,2,4,128,256]{4,3,2,1,0:T(8,128)(2,1)S(1)} %copy-done.1), kind=kLoop, calls=%fused_computation.24 | loop fusion | bytes 2097152 | tf_op jit(solution)/shard_map/slice | solution.py:383
  10.0 1.8 %collective-permute-start.1 = (bf16[2,1,4,128,256]{4,3,2,1,0:T(8,128)(2,1)}, bf16[2,1,4,128,256]{4,3,2,1,0:T(8,128)(2,1)S(1)}, u32[]{:S(2)}, u32[]{:S(2)}) collective-permute-start(bf16[2,1,4,128,256]{4,3,2,1,0:T(8,128)(2,1)} %get-tuple-element.71), channel_id=1, source_target_pairs={{4,0},{8,4},{12,8},{16,12},{20,16},{24,20},{28,24},{0,28},{5,1},{9... | collective-permute-start | bytes 1572872 | tf_op jit(solution)/shard_map/ppermute | solution.py:331
  11.9 0.1 fusion.1
  12.1 0.2 mul.24
  12.5 0.7 %collective-permute-done.3 = bf16[2,2,1,128,256]{4,3,2,1,0:T(8,128)(2,1)S(1)} collective-permute-done((bf16[2,2,1,128,256]{4,3,2,1,0:T(8,128)(2,1)S(1)}, bf16[2,2,1,128,256]{4,3,2,1,0:T(8,128)(2,1)S(1)}, u32[]{:S(2)}, u32[]{:S(2)}) %collective-permute-start.3) | collective-permute-done | bytes 262176 | tf_op jit(solution)/shard_map/ppermute | solution.py:331
  13.3 1.5 %collective-permute-done.2 = bf16[2,2,1,128,256]{4,3,2,1,0:T(8,128)(2,1)S(1)} collective-permute-done((bf16[2,2,1,128,256]{4,3,2,1,0:T(8,128)(2,1)}, bf16[2,2,1,128,256]{4,3,2,1,0:T(8,128)(2,1)S(1)}, u32[]{:S(2)}, u32[]{:S(2)}) %collective-permute-start.2) | collective-permute-done | bytes 262176 | tf_op jit(solution)/shard_map/ppermute | solution.py:331
  14.8 0.7 %pad_maximum_fusion.3 = bf16[2,1,2,128,256]{4,3,2,1,0:T(8,128)(2,1)} fusion(bf16[2,1,1,128,256]{4,3,2,1,0:T(8,128)(2,1)S(1)} %get-tuple-element.76, bf16[2,1,1,128,256]{4,3,2,1,0:T(8,128)(2,1)S(1)} %get-tuple-element.74), kind=kLoop, calls=%fused_computation.6 | loop fusion | flops 131072 | bytes 524288 | tf_op jit(solution)/shard_map/concatenate | solution.py:384
  15.5 0.7 %pad_maximum_fusion.4 = bf16[2,1,2,128,256]{4,3,2,1,0:T(8,128)(2,1)} fusion(bf16[2,1,1,128,256]{4,3,2,1,0:T(8,128)(2,1)S(1)} %get-tuple-element.75, bf16[2,1,1,128,256]{4,3,2,1,0:T(8,128)(2,1)S(1)} %get-tuple-element.73), kind=kLoop, calls=%fused_computation.7 | loop fusion | flops 131072 | bytes 524288 | tf_op jit(solution)/shard_map/concatenate | solution.py:385
  16.3 2.6 %collective-permute-start.5 = (bf16[2,1,2,128,256]{4,3,2,1,0:T(8,128)(2,1)}, bf16[2,1,2,128,256]{4,3,2,1,0:T(8,128)(2,1)S(1)}, u32[]{:S(2)}, u32[]{:S(2)}) collective-permute-start(bf16[2,1,2,128,256]{4,3,2,1,0:T(8,128)(2,1)} %pad_maximum_fusion.4), channel_id=1, source_target_pairs={{4,0},{8,4},{12,8},{16,12},{20,16},{24,20},{28,24},{0,28},{5,1},{9... | collective-permute-start | bytes 786440 | tf_op jit(solution)/shard_map/ppermute | solution.py:331
  18.9 0.9 %mul.21 = bf16[32,8,144]{2,1,0:T(8,128)(2,1)} reshape(bf16[32,1152]{1,0:T(8,128)(2,1)S(1)} %fusion.1) | data formatting | bytes 147456 | tf_op jit(solution)/shard_map/mul | solution.py:399
  20.0 0.9 %copy.24 = bf16[32,8,144]{2,0,1:T(8,128)(2,1)S(1)} copy(bf16[32,8,144]{2,1,0:T(8,128)(2,1)} %mul.21) | data formatting | bytes 147456 | tf_op jit(solution)/shard_map/mul | solution.py:399
  21.0 10.4 %collective-permute-done.4 = bf16[2,1,2,128,256]{4,3,2,1,0:T(8,128)(2,1)S(1)} collective-permute-done((bf16[2,1,2,128,256]{4,3,2,1,0:T(8,128)(2,1)}, bf16[2,1,2,128,256]{4,3,2,1,0:T(8,128)(2,1)S(1)}, u32[]{:S(2)}, u32[]{:S(2)}) %collective-permute-start.4) | collective-permute-done | bytes 262176 | tf_op jit(solution)/shard_map/ppermute | solution.py:331
  31.5 3.4 %observe.1 = (bf16[130,48,256]{2,1,0:T(8,128)(2,1)S(1)}, bf16[80,256]{1,0:T(8,128)(2,1)S(1)}) custom-call(bf16[16,128,256]{2,1,0:T(8,128)(2,1)S(1)} %bitcast.28, bf16[8,128,256]{2,1,0:T(8,128)(2,1)S(1)} %bitcast.33, bf16[8,128,256]{2,1,0:T(8,128)(2,1)S(1)} %bitcast.32, bf16[4,128,256]{2,1,0:T(8,128)(2,1)S(1)} %bitcast.31, bf16[4,128,256]{2,1,0:T(8,128)(2,1)S(1)} %bitcast.30, ...), custom_call_target="tpu_custom_call" | custom-call | tf_op jit(solution)/shard_map/observe/pallas_call | solution.py:421
  34.9 2.6 %collective-permute-start.6 = (bf16[1,80,256]{2,1,0:T(8,128)(2,1)S(1)}, bf16[1,80,256]{2,1,0:T(8,128)(2,1)S(1)}, u32[]{:S(2)}, u32[]{:S(2)}) collective-permute-start(bf16[1,80,256]{2,1,0:T(8,128)(2,1)S(1)} %bitcast.36), channel_id=1, source_target_pairs={{0,2},{1,3},{2,0},{3,1},{4,6},{5,7},{6,4},{7,5},{8,10},{9,11},{10,... | collective-permute-start | bytes 122888 | tf_op jit(solution)/shard_map/ppermute | solution.py:340
  37.5 2.0 %saturate.4 = (bf16[8,16,256]{2,1,0:T(8,128)(2,1)S(1)}, f32[8,16,1]{2,1,0:T(8,128)S(1)}) custom-call(bf16[130,48,256]{2,1,0:T(8,128)(2,1)S(1)} %get-tuple-element.55.packed, bf16[256,160]{1,0:T(8,128)(2,1)S(1)} %maximum_maximum_fusion.weights, bf16[128,128]{1,0:T(8,128)(2,1)S(1)} %copy-done.2, f32[8,128]{1,0:T(8,128)S(1)} %convert_element_type.5.mask, ...), custom_call_target="tpu_custom_call" | custom-call | flops 536870912 | bytes 4194304 | tf_op jit(solution)/shard_map/saturate/pallas_call | solution.py:439
  39.6 0.3 collective-permute-done.6
  39.9 1.6 %collective-permute-start.7 = (bf16[2,80,256]{2,1,0:T(8,128)(2,1)S(1)}, bf16[2,80,256]{2,1,0:T(8,128)(2,1)S(1)}, u32[]{:S(2)}, u32[]{:S(2)}) collective-permute-start(bf16[2,80,256]{2,1,0:T(8,128)(2,1)S(1)} %pad_maximum_fusion.6), channel_id=1, source_target_pairs={{0,1},{1,0},{2,3},{3,2},{4,5},{5,4},{6,7},{7,6},{8,9},{9,8},{10,11... | collective-permute-start | bytes 245768 | tf_op jit(solution)/shard_map/ppermute | solution.py:340
  41.5 2.0 %saturate.5 = (bf16[8,16,256]{2,1,0:T(8,128)(2,1)S(1)}, f32[8,16,1]{2,1,0:T(8,128)S(1)}) custom-call(bf16[130,48,256]{2,1,0:T(8,128)(2,1)S(1)} %get-tuple-element.55.packed, bf16[256,160]{1,0:T(8,128)(2,1)S(1)} %maximum_maximum_fusion.weights, bf16[128,128]{1,0:T(8,128)(2,1)S(1)} %copy-done.2, f32[8,128]{1,0:T(8,128)S(1)} %convert_element_type.5.mask, ...), custom_call_target="tpu_custom_call" | custom-call | flops 536870912 | bytes 4194304 | tf_op jit(solution)/shard_map/saturate/pallas_call | solution.py:439
  43.5 0.9 %collective-permute-done.7 = bf16[2,80,256]{2,1,0:T(8,128)(2,1)S(1)} collective-permute-done((bf16[2,80,256]{2,1,0:T(8,128)(2,1)S(1)}, bf16[2,80,256]{2,1,0:T(8,128)(2,1)S(1)}, u32[]{:S(2)}, u32[]{:S(2)}) %collective-permute-start.7) | collective-permute-done | bytes 81952 | tf_op jit(solution)/shard_map/ppermute | solution.py:340
  44.4 0.6 collective-permute-start.8
  45.0 4.5 %saturate.6 = (bf16[8,48,256]{2,1,0:T(8,128)(2,1)S(1)}, f32[8,48,1]{2,1,0:T(8,128)S(1)}) custom-call(bf16[130,48,256]{2,1,0:T(8,128)(2,1)S(1)} %get-tuple-element.55.packed, bf16[256,160]{1,0:T(8,128)(2,1)S(1)} %maximum_maximum_fusion.weights, bf16[128,128]{1,0:T(8,128)(2,1)S(1)} %copy-done.2, f32[8,128]{1,0:T(8,128)S(1)} %convert_element_type.5.mask, ...), custom_call_target="tpu_custom_call" | custom-call | flops 1610612736 | bytes 4194304 | tf_op jit(solution)/shard_map/saturate/pallas_call | solution.py:439
  49.6 0.2 collective-permute-done.8
  49.8 0.7 %collective-permute-start.9 = (bf16[8,80,256]{2,1,0:T(8,128)(2,1)S(1)}, bf16[8,80,256]{2,1,0:T(8,128)(2,1)S(1)}, u32[]{:S(2)}, u32[]{:S(2)}) collective-permute-start(bf16[8,80,256]{2,1,0:T(8,128)(2,1)S(1)} %pad_maximum_fusion.2), channel_id=1, source_target_pairs={{0,16},{4,20},{8,24},{12,28},{16,0},{20,4},{24,8},{28,12},{1,17},{... | collective-permute-start | bytes 983048 | tf_op jit(solution)/shard_map/ppermute | solution.py:340
  50.5 4.5 %saturate.7 = (bf16[8,48,256]{2,1,0:T(8,128)(2,1)S(1)}, f32[8,48,1]{2,1,0:T(8,128)S(1)}) custom-call(bf16[130,48,256]{2,1,0:T(8,128)(2,1)S(1)} %get-tuple-element.55.packed, bf16[256,160]{1,0:T(8,128)(2,1)S(1)} %maximum_maximum_fusion.weights, bf16[128,128]{1,0:T(8,128)(2,1)S(1)} %copy-done.2, f32[8,128]{1,0:T(8,128)S(1)} %convert_element_type.5.mask, ...), custom_call_target="tpu_custom_call" | custom-call | flops 1610612736 | bytes 4194304 | tf_op jit(solution)/shard_map/saturate/pallas_call | solution.py:439
  55.1 1.9 %collective-permute-done.9 = bf16[8,80,256]{2,1,0:T(8,128)(2,1)S(1)} collective-permute-done((bf16[8,80,256]{2,1,0:T(8,128)(2,1)S(1)}, bf16[8,80,256]{2,1,0:T(8,128)(2,1)S(1)}, u32[]{:S(2)}, u32[]{:S(2)}) %collective-permute-start.9) | collective-permute-done | bytes 327712 | tf_op jit(solution)/shard_map/ppermute | solution.py:340
  57.1 0.9 %moments.1 = (bf16[16,128,256]{2,1,0:T(8,128)(2,1)S(1)}, f32[16,128,1]{2,1,0:T(8,128)S(1)}) custom-call(bf16[16,128,256]{2,1,0:T(8,128)(2,1)S(1)} %bitcast.29), custom_call_target="tpu_custom_call" | custom-call | tf_op jit(solution)/shard_map/moments/pallas_call | solution.py:411
  58.0 1.2 %collective-permute-done.10 = bf16[16,80,256]{2,1,0:T(8,128)(2,1)S(1)} collective-permute-done((bf16[16,80,256]{2,1,0:T(8,128)(2,1)S(1)}, bf16[16,80,256]{2,1,0:T(8,128)(2,1)S(1)}, u32[]{:S(2)}, u32[]{:S(2)}) %collective-permute-start.10) | collective-permute-done | bytes 655392 | tf_op jit(solution)/shard_map/ppermute | solution.py:340
  59.2 0.1 pad_maximum_fusion.refs_0_
  59.3 10.0 %update.1 = bf16[24,128,256]{2,1,0:T(8,128)(2,1)} custom-call(bf16[32,80,256]{2,1,0:T(8,128)(2,1)S(1)} %pad_maximum_fusion.refs_0_, bf16[16,128,256]{2,1,0:T(8,128)(2,1)S(1)} %get-tuple-element.59.refs_1_, f32[16,128,1]{2,1,0:T(8,128)S(1)} %get-tuple-element.60.refs_2_, bf16[8,16,256]{2,1,0:T(8,128)(2,1)S(1)} %get-tuple-element.61.refs_3_, ...), custom_call_target="tpu_custom_call" | custom-call | tf_op jit(solution)/shard_map/update/pallas_call | solution.py:470
  (48 shorter events, 0.9 us)
Async XLA Ops:
  0.0 11.9 %copy-start = (bf16[54,32]{0,1:T(8,128)(2,1)S(1)}, bf16[54,32]{0,1:T(8,128)(2,1)}, u32[]{:S(2)}) copy-start(bf16[54,32]{0,1:T(8,128)(2,1)} %param.13) | copy-start | bytes 10372
  0.0 8.9 %copy-start.1 = (bf16[2,2,4,128,256]{4,3,2,1,0:T(8,128)(2,1)S(1)}, bf16[2,2,4,128,256]{4,3,2,1,0:T(8,128)(2,1)}, u32[]{:S(2)}) copy-start(bf16[2,2,4,128,256]{4,3,2,1,0:T(8,128)(2,1)} %param.11) | copy-start | bytes 3145732
  1.9 9.9 %copy-start.7 = (f32[32]{0:T(128)S(1)}, f32[32]{0:T(128)}, u32[]{:S(2)}) copy-start(f32[32]{0:T(128)} %param.14) | copy-start | bytes 388
  1.9 10.0 %copy-start.6 = (bf16[54,1152]{1,0:T(8,128)(2,1)S(1)}, bf16[54,1152]{1,0:T(8,128)(2,1)}, u32[]{:S(2)}) copy-start(bf16[54,1152]{1,0:T(8,128)(2,1)} %constant.12.clone) | copy-start | bytes 373252
  1.9 11.3 %collective-permute-start.3 = (bf16[2,2,1,128,256]{4,3,2,1,0:T(8,128)(2,1)S(1)}, bf16[2,2,1,128,256]{4,3,2,1,0:T(8,128)(2,1)S(1)}, u32[]{:S(2)}, u32[]{:S(2)}) collective-permute-start(bf16[2,2,1,128,256]{4,3,2,1,0:T(8,128)(2,1)S(1)} %get-tuple-element.69), channel_id=1, source_target_pairs={{1,0},{2,1},{3,2},{5,4},{6,5},{7,6},{9,8},{10,9},{11,10},{13,12},{... | collective-permute-start | bytes 786440 | tf_op jit(solution)/shard_map/ppermute | solution.py:331
  3.3 9.2 %copy-start.10 = (f32[32]{0:T(128)S(1)}, f32[32]{0:T(128)}, u32[]{:S(2)}) copy-start(f32[32]{0:T(128)} %param.15) | copy-start | bytes 388
  3.3 11.4 %collective-permute-start.2 = (bf16[2,2,1,128,256]{4,3,2,1,0:T(8,128)(2,1)}, bf16[2,2,1,128,256]{4,3,2,1,0:T(8,128)(2,1)S(1)}, u32[]{:S(2)}, u32[]{:S(2)}) collective-permute-start(bf16[2,2,1,128,256]{4,3,2,1,0:T(8,128)(2,1)} %get-tuple-element.70), channel_id=1, source_target_pairs={{0,1},{1,2},{2,3},{4,5},{5,6},{6,7},{8,9},{9,10},{10,11},{12,13},{... | collective-permute-start | bytes 786440 | tf_op jit(solution)/shard_map/ppermute | solution.py:331
  10.0 21.5 %collective-permute-start.1 = (bf16[2,1,4,128,256]{4,3,2,1,0:T(8,128)(2,1)}, bf16[2,1,4,128,256]{4,3,2,1,0:T(8,128)(2,1)S(1)}, u32[]{:S(2)}, u32[]{:S(2)}) collective-permute-start(bf16[2,1,4,128,256]{4,3,2,1,0:T(8,128)(2,1)} %get-tuple-element.71), channel_id=1, source_target_pairs={{4,0},{8,4},{12,8},{16,12},{20,16},{24,20},{28,24},{0,28},{5,1},{9... | collective-permute-start | bytes 1572872 | tf_op jit(solution)/shard_map/ppermute | solution.py:331
  11.7 19.7 %collective-permute-start = (bf16[2,1,4,128,256]{4,3,2,1,0:T(8,128)(2,1)}, bf16[2,1,4,128,256]{4,3,2,1,0:T(8,128)(2,1)S(1)}, u32[]{:S(2)}, u32[]{:S(2)}) collective-permute-start(bf16[2,1,4,128,256]{4,3,2,1,0:T(8,128)(2,1)} %get-tuple-element.72), channel_id=1, source_target_pairs={{0,4},{4,8},{8,12},{12,16},{16,20},{20,24},{24,28},{28,0},{1,5},{5... | collective-permute-start | bytes 1572872 | tf_op jit(solution)/shard_map/ppermute | solution.py:331
  12.0 6.9 %copy-start.8 = (f32[64]{0:T(128)S(1)}, f32[64]{0:T(128)}, u32[]{:S(2)}) copy-start(f32[64]{0:T(128)} %param.17) | copy-start | bytes 772
  12.1 6.8 %copy-start.9 = (f32[64]{0:T(128)S(1)}, f32[64]{0:T(128)}, u32[]{:S(2)}) copy-start(f32[64]{0:T(128)} %param.18) | copy-start | bytes 772
  12.4 7.4 %copy-start.4 = (s32[2,4,128]{2,1,0:T(4,128)S(1)}, s32[2,4,128]{2,1,0:T(4,128)}, u32[]{:S(2)}) copy-start(s32[2,4,128]{2,1,0:T(4,128)} %param.12) | copy-start | bytes 12292
  13.3 18.2 %copy-start.3 = (bf16[256,256]{1,0:T(8,128)(2,1)S(1)}, bf16[256,256]{1,0:T(8,128)(2,1)}, u32[]{:S(2)}) copy-start(bf16[256,256]{1,0:T(8,128)(2,1)} %constant.13.clone.swap_in) | copy-start | bytes 393220
  13.3 18.2 %copy-start.5 = (s32[64]{0:T(128)S(1)}, s32[64]{0:T(128)}, u32[]{:S(2)}) copy-start(s32[64]{0:T(128)} %cells.1) | copy-start | bytes 772
  15.5 15.9 %collective-permute-start.4 = (bf16[2,1,2,128,256]{4,3,2,1,0:T(8,128)(2,1)}, bf16[2,1,2,128,256]{4,3,2,1,0:T(8,128)(2,1)S(1)}, u32[]{:S(2)}, u32[]{:S(2)}) collective-permute-start(bf16[2,1,2,128,256]{4,3,2,1,0:T(8,128)(2,1)} %pad_maximum_fusion.3), channel_id=1, source_target_pairs={{0,4},{4,8},{8,12},{12,16},{16,20},{20,24},{24,28},{28,0},{1,5},{5... | collective-permute-start | bytes 786440 | tf_op jit(solution)/shard_map/ppermute | solution.py:331
  16.3 15.2 %collective-permute-start.5 = (bf16[2,1,2,128,256]{4,3,2,1,0:T(8,128)(2,1)}, bf16[2,1,2,128,256]{4,3,2,1,0:T(8,128)(2,1)S(1)}, u32[]{:S(2)}, u32[]{:S(2)}) collective-permute-start(bf16[2,1,2,128,256]{4,3,2,1,0:T(8,128)(2,1)} %pad_maximum_fusion.4), channel_id=1, source_target_pairs={{4,0},{8,4},{12,8},{16,12},{20,16},{24,20},{28,24},{0,28},{5,1},{9... | collective-permute-start | bytes 786440 | tf_op jit(solution)/shard_map/ppermute | solution.py:331
  31.5 6.1 %copy-start.2 = (bf16[128,128]{1,0:T(8,128)(2,1)S(1)}, bf16[128,128]{1,0:T(8,128)(2,1)}, u32[]{:S(2)}) copy-start(bf16[128,128]{1,0:T(8,128)(2,1)} %constant.14.clone.swap_out) | copy-start | bytes 98308
  34.9 5.0 %collective-permute-start.6 = (bf16[1,80,256]{2,1,0:T(8,128)(2,1)S(1)}, bf16[1,80,256]{2,1,0:T(8,128)(2,1)S(1)}, u32[]{:S(2)}, u32[]{:S(2)}) collective-permute-start(bf16[1,80,256]{2,1,0:T(8,128)(2,1)S(1)} %bitcast.36), channel_id=1, source_target_pairs={{0,2},{1,3},{2,0},{3,1},{4,6},{5,7},{6,4},{7,5},{8,10},{9,11},{10,... | collective-permute-start | bytes 122888 | tf_op jit(solution)/shard_map/ppermute | solution.py:340
  39.9 4.5 %collective-permute-start.7 = (bf16[2,80,256]{2,1,0:T(8,128)(2,1)S(1)}, bf16[2,80,256]{2,1,0:T(8,128)(2,1)S(1)}, u32[]{:S(2)}, u32[]{:S(2)}) collective-permute-start(bf16[2,80,256]{2,1,0:T(8,128)(2,1)S(1)} %pad_maximum_fusion.6), channel_id=1, source_target_pairs={{0,1},{1,0},{2,3},{3,2},{4,5},{5,4},{6,7},{7,6},{8,9},{9,8},{10,11... | collective-permute-start | bytes 245768 | tf_op jit(solution)/shard_map/ppermute | solution.py:340
  44.4 5.4 %collective-permute-start.8 = (bf16[4,80,256]{2,1,0:T(8,128)(2,1)S(1)}, bf16[4,80,256]{2,1,0:T(8,128)(2,1)S(1)}, u32[]{:S(2)}, u32[]{:S(2)}) collective-permute-start(bf16[4,80,256]{2,1,0:T(8,128)(2,1)S(1)} %pad_maximum_fusion.5), channel_id=1, source_target_pairs={{0,8},{4,12},{8,0},{12,4},{16,24},{20,28},{24,16},{28,20},{1,9},{5... | collective-permute-start | bytes 491528 | tf_op jit(solution)/shard_map/ppermute | solution.py:340
  49.8 7.1 %collective-permute-start.9 = (bf16[8,80,256]{2,1,0:T(8,128)(2,1)S(1)}, bf16[8,80,256]{2,1,0:T(8,128)(2,1)S(1)}, u32[]{:S(2)}, u32[]{:S(2)}) collective-permute-start(bf16[8,80,256]{2,1,0:T(8,128)(2,1)S(1)} %pad_maximum_fusion.2), channel_id=1, source_target_pairs={{0,16},{4,20},{8,24},{12,28},{16,0},{20,4},{24,8},{28,12},{1,17},{... | collective-permute-start | bytes 983048 | tf_op jit(solution)/shard_map/ppermute | solution.py:340
  57.0 2.2 %collective-permute-start.10 = (bf16[16,80,256]{2,1,0:T(8,128)(2,1)S(1)}, bf16[16,80,256]{2,1,0:T(8,128)(2,1)S(1)}, u32[]{:S(2)}, u32[]{:S(2)}) collective-permute-start(bf16[16,80,256]{2,1,0:T(8,128)(2,1)S(1)} %pad_maximum_fusion.1), channel_id=1, source_target_pairs={{0,4},{4,0},{8,12},{12,8},{16,20},{20,16},{24,28},{28,24},{1,5},{5... | collective-permute-start | bytes 1966088 | tf_op jit(solution)/shard_map/ppermute | solution.py:340

commit v2 on v1

--- a/solution.py
+++ b/solution.py
@@ -258,7 +258,7 @@
     identity = jnp.where(sub == lane, 1.0, 0.0)
     if gathered:
         devices, observed = pay.shape[0], pay.shape[1] - PAY_ROWS
-        group = max(1, 256 // observed)
+        group = max(1, 2048 // observed)
         total = identity
         for d in range(0, devices, group):
             block = pay[d : d + group, 0:observed, :].reshape(-1, members)

time: 69.5 us -> 69.4 us (level)
  no operation moved by 1% of the time
where the time goes in v2:
time: 69.4 us; the launch traced here: 69.2 us
  Pallas kernels  27.3 us (39%)
  starting transfers between devices  17.1 us (25%)
  waiting for transfers between devices  17 us (24%)
  local copies, waits for them, and re-layouts  5.4 us (8%)
  other arithmetic  1.94 us (3%)
    pallas_call x4, Pallas kernels, saturate(): pl.pallas_call(functools.partial(saturate_kernel, starts[n]), out_shape=m...  13.1 us
    ppermute x6, waiting for transfers between devices, shift(): return lax.ppermute(value, axis, pairs)  12.7 us
    ppermute x6, starting transfers between devices, shift(): return lax.ppermute(value, axis, pairs)  11.4 us
    pallas_call x1, Pallas kernels, shards(): pl.pallas_call(functools.partial(update_kernel, gathered), out_shape=jax....  9.95 us
    ppermute x5, starting transfers between devices, gather_rows(): other = lax.ppermute(block, axis, [(i, i ^ bit) for i in range(count)])  5.74 us
    ppermute x5, waiting for transfers between devices, gather_rows(): other = lax.ppermute(block, axis, [(i, i ^ bit) for i in range(count)])  4.38 us
    pallas_call x1, Pallas kernels, shards(): pl.pallas_call(observe_kernel, out_shape=(jax.ShapeDtypeStruct((lanes + 2...  3.39 us
    mul x3, local copies, waits for them, and re-layouts, shards(): 0.5 * taps  1.99 us
  transfers between devices with their start and end apart: 11, of which 8 were waited for; matrix products, arithmetic and copies ran while one was open for 8% of the time, Pallas kernels for 20%

profile of v2, /device:TPU:0, one launch (start us, length us, event | category | flops | bytes accessed | tf_op | source)
XLA Modules:
  0.0 69.2 jit_solution(5081161077444973715)
XLA Ops:
  0.0 1.9 %fusion.5 = (bf16[2,2,1,128,256]{4,3,2,1,0:T(8,128)(2,1)S(1)}, bf16[2,2,1,128,256]{4,3,2,1,0:T(8,128)(2,1)}) fusion(bf16[2,2,4,128,256]{4,3,2,1,0:T(8,128)(2,1)} %param.11), kind=kLoop, calls=%fused_computation.23 | loop fusion | bytes 1048576 | tf_op jit(solution)/shard_map/slice | solution.py:381
  1.9 1.4 %collective-permute-start.3 = (bf16[2,2,1,128,256]{4,3,2,1,0:T(8,128)(2,1)S(1)}, bf16[2,2,1,128,256]{4,3,2,1,0:T(8,128)(2,1)S(1)}, u32[]{:S(2)}, u32[]{:S(2)}) collective-permute-start(bf16[2,2,1,128,256]{4,3,2,1,0:T(8,128)(2,1)S(1)} %get-tuple-element.69), channel_id=1, source_target_pairs={{1,0},{2,1},{3,2},{5,4},{6,5},{7,6},{9,8},{10,9},{11,10},{13,12},{... | collective-permute-start | bytes 786440 | tf_op jit(solution)/shard_map/ppermute | solution.py:331
  3.3 5.6 %collective-permute-start.2 = (bf16[2,2,1,128,256]{4,3,2,1,0:T(8,128)(2,1)}, bf16[2,2,1,128,256]{4,3,2,1,0:T(8,128)(2,1)S(1)}, u32[]{:S(2)}, u32[]{:S(2)}) collective-permute-start(bf16[2,2,1,128,256]{4,3,2,1,0:T(8,128)(2,1)} %get-tuple-element.70), channel_id=1, source_target_pairs={{0,1},{1,2},{2,3},{4,5},{5,6},{6,7},{8,9},{9,10},{10,11},{12,13},{... | collective-permute-start | bytes 786440 | tf_op jit(solution)/shard_map/ppermute | solution.py:331
  8.9 1.1 %fusion.6 = (bf16[2,1,4,128,256]{4,3,2,1,0:T(8,128)(2,1)}, bf16[2,1,4,128,256]{4,3,2,1,0:T(8,128)(2,1)}) fusion(bf16[2,2,4,128,256]{4,3,2,1,0:T(8,128)(2,1)S(1)} %copy-done.1), kind=kLoop, calls=%fused_computation.24 | loop fusion | bytes 2097152 | tf_op jit(solution)/shard_map/slice | solution.py:383
  10.0 1.8 %collective-permute-start.1 = (bf16[2,1,4,128,256]{4,3,2,1,0:T(8,128)(2,1)}, bf16[2,1,4,128,256]{4,3,2,1,0:T(8,128)(2,1)S(1)}, u32[]{:S(2)}, u32[]{:S(2)}) collective-permute-start(bf16[2,1,4,128,256]{4,3,2,1,0:T(8,128)(2,1)} %get-tuple-element.71), channel_id=1, source_target_pairs={{4,0},{8,4},{12,8},{16,12},{20,16},{24,20},{28,24},{0,28},{5,1},{9... | collective-permute-start | bytes 1572872 | tf_op jit(solution)/shard_map/ppermute | solution.py:331
  11.9 0.1 fusion.1
  12.1 0.2 mul.24
  12.5 0.7 %collective-permute-done.3 = bf16[2,2,1,128,256]{4,3,2,1,0:T(8,128)(2,1)S(1)} collective-permute-done((bf16[2,2,1,128,256]{4,3,2,1,0:T(8,128)(2,1)S(1)}, bf16[2,2,1,128,256]{4,3,2,1,0:T(8,128)(2,1)S(1)}, u32[]{:S(2)}, u32[]{:S(2)}) %collective-permute-start.3) | collective-permute-done | bytes 262176 | tf_op jit(solution)/shard_map/ppermute | solution.py:331
  13.3 1.5 %collective-permute-done.2 = bf16[2,2,1,128,256]{4,3,2,1,0:T(8,128)(2,1)S(1)} collective-permute-done((bf16[2,2,1,128,256]{4,3,2,1,0:T(8,128)(2,1)}, bf16[2,2,1,128,256]{4,3,2,1,0:T(8,128)(2,1)S(1)}, u32[]{:S(2)}, u32[]{:S(2)}) %collective-permute-start.2) | collective-permute-done | bytes 262176 | tf_op jit(solution)/shard_map/ppermute | solution.py:331
  14.8 0.7 %pad_maximum_fusion.3 = bf16[2,1,2,128,256]{4,3,2,1,0:T(8,128)(2,1)} fusion(bf16[2,1,1,128,256]{4,3,2,1,0:T(8,128)(2,1)S(1)} %get-tuple-element.76, bf16[2,1,1,128,256]{4,3,2,1,0:T(8,128)(2,1)S(1)} %get-tuple-element.74), kind=kLoop, calls=%fused_computation.6 | loop fusion | flops 131072 | bytes 524288 | tf_op jit(solution)/shard_map/concatenate | solution.py:384
  15.5 0.7 %pad_maximum_fusion.4 = bf16[2,1,2,128,256]{4,3,2,1,0:T(8,128)(2,1)} fusion(bf16[2,1,1,128,256]{4,3,2,1,0:T(8,128)(2,1)S(1)} %get-tuple-element.75, bf16[2,1,1,128,256]{4,3,2,1,0:T(8,128)(2,1)S(1)} %get-tuple-element.73), kind=kLoop, calls=%fused_computation.7 | loop fusion | flops 131072 | bytes 524288 | tf_op jit(solution)/shard_map/concatenate | solution.py:385
  16.3 2.6 %collective-permute-start.5 = (bf16[2,1,2,128,256]{4,3,2,1,0:T(8,128)(2,1)}, bf16[2,1,2,128,256]{4,3,2,1,0:T(8,128)(2,1)S(1)}, u32[]{:S(2)}, u32[]{:S(2)}) collective-permute-start(bf16[2,1,2,128,256]{4,3,2,1,0:T(8,128)(2,1)} %pad_maximum_fusion.4), channel_id=1, source_target_pairs={{4,0},{8,4},{12,8},{16,12},{20,16},{24,20},{28,24},{0,28},{5,1},{9... | collective-permute-start | bytes 786440 | tf_op jit(solution)/shard_map/ppermute | solution.py:331
  18.9 0.9 %mul.21 = bf16[32,8,144]{2,1,0:T(8,128)(2,1)} reshape(bf16[32,1152]{1,0:T(8,128)(2,1)S(1)} %fusion.1) | data formatting | bytes 147456 | tf_op jit(solution)/shard_map/mul | solution.py:399
  20.0 0.9 %copy.24 = bf16[32,8,144]{2,0,1:T(8,128)(2,1)S(1)} copy(bf16[32,8,144]{2,1,0:T(8,128)(2,1)} %mul.21) | data formatting | bytes 147456 | tf_op jit(solution)/shard_map/mul | solution.py:399
  21.0 10.4 %collective-permute-done.4 = bf16[2,1,2,128,256]{4,3,2,1,0:T(8,128)(2,1)S(1)} collective-permute-done((bf16[2,1,2,128,256]{4,3,2,1,0:T(8,128)(2,1)}, bf16[2,1,2,128,256]{4,3,2,1,0:T(8,128)(2,1)S(1)}, u32[]{:S(2)}, u32[]{:S(2)}) %collective-permute-start.4) | collective-permute-done | bytes 262176 | tf_op jit(solution)/shard_map/ppermute | solution.py:331
  31.5 3.4 %observe.1 = (bf16[130,48,256]{2,1,0:T(8,128)(2,1)S(1)}, bf16[80,256]{1,0:T(8,128)(2,1)S(1)}) custom-call(bf16[16,128,256]{2,1,0:T(8,128)(2,1)S(1)} %bitcast.28, bf16[8,128,256]{2,1,0:T(8,128)(2,1)S(1)} %bitcast.33, bf16[8,128,256]{2,1,0:T(8,128)(2,1)S(1)} %bitcast.32, bf16[4,128,256]{2,1,0:T(8,128)(2,1)S(1)} %bitcast.31, bf16[4,128,256]{2,1,0:T(8,128)(2,1)S(1)} %bitcast.30, ...), custom_call_target="tpu_custom_call" | custom-call | tf_op jit(solution)/shard_map/observe/pallas_call | solution.py:421
  34.9 2.6 %collective-permute-start.6 = (bf16[1,80,256]{2,1,0:T(8,128)(2,1)S(1)}, bf16[1,80,256]{2,1,0:T(8,128)(2,1)S(1)}, u32[]{:S(2)}, u32[]{:S(2)}) collective-permute-start(bf16[1,80,256]{2,1,0:T(8,128)(2,1)S(1)} %bitcast.36), channel_id=1, source_target_pairs={{0,2},{1,3},{2,0},{3,1},{4,6},{5,7},{6,4},{7,5},{8,10},{9,11},{10,... | collective-permute-start | bytes 122888 | tf_op jit(solution)/shard_map/ppermute | solution.py:340
  37.5 2.0 %saturate.4 = (bf16[8,16,256]{2,1,0:T(8,128)(2,1)S(1)}, f32[8,16,1]{2,1,0:T(8,128)S(1)}) custom-call(bf16[130,48,256]{2,1,0:T(8,128)(2,1)S(1)} %get-tuple-element.55.packed, bf16[256,160]{1,0:T(8,128)(2,1)S(1)} %maximum_maximum_fusion.weights, bf16[128,128]{1,0:T(8,128)(2,1)S(1)} %copy-done.2, f32[8,128]{1,0:T(8,128)S(1)} %convert_element_type.5.mask, ...), custom_call_target="tpu_custom_call" | custom-call | flops 536870912 | bytes 4194304 | tf_op jit(solution)/shard_map/saturate/pallas_call | solution.py:439
  39.6 0.3 collective-permute-done.6
  39.9 1.6 %collective-permute-start.7 = (bf16[2,80,256]{2,1,0:T(8,128)(2,1)S(1)}, bf16[2,80,256]{2,1,0:T(8,128)(2,1)S(1)}, u32[]{:S(2)}, u32[]{:S(2)}) collective-permute-start(bf16[2,80,256]{2,1,0:T(8,128)(2,1)S(1)} %pad_maximum_fusion.6), channel_id=1, source_target_pairs={{0,1},{1,0},{2,3},{3,2},{4,5},{5,4},{6,7},{7,6},{8,9},{9,8},{10,11... | collective-permute-start | bytes 245768 | tf_op jit(solution)/shard_map/ppermute | solution.py:340
  41.5 2.0 %saturate.5 = (bf16[8,16,256]{2,1,0:T(8,128)(2,1)S(1)}, f32[8,16,1]{2,1,0:T(8,128)S(1)}) custom-call(bf16[130,48,256]{2,1,0:T(8,128)(2,1)S(1)} %get-tuple-element.55.packed, bf16[256,160]{1,0:T(8,128)(2,1)S(1)} %maximum_maximum_fusion.weights, bf16[128,128]{1,0:T(8,128)(2,1)S(1)} %copy-done.2, f32[8,128]{1,0:T(8,128)S(1)} %convert_element_type.5.mask, ...), custom_call_target="tpu_custom_call" | custom-call | flops 536870912 | bytes 4194304 | tf_op jit(solution)/shard_map/saturate/pallas_call | solution.py:439
  43.5 0.8 %collective-permute-done.7 = bf16[2,80,256]{2,1,0:T(8,128)(2,1)S(1)} collective-permute-done((bf16[2,80,256]{2,1,0:T(8,128)(2,1)S(1)}, bf16[2,80,256]{2,1,0:T(8,128)(2,1)S(1)}, u32[]{:S(2)}, u32[]{:S(2)}) %collective-permute-start.7) | collective-permute-done | bytes 81952 | tf_op jit(solution)/shard_map/ppermute | solution.py:340
  44.4 0.6 collective-permute-start.8
  45.0 4.5 %saturate.6 = (bf16[8,48,256]{2,1,0:T(8,128)(2,1)S(1)}, f32[8,48,1]{2,1,0:T(8,128)S(1)}) custom-call(bf16[130,48,256]{2,1,0:T(8,128)(2,1)S(1)} %get-tuple-element.55.packed, bf16[256,160]{1,0:T(8,128)(2,1)S(1)} %maximum_maximum_fusion.weights, bf16[128,128]{1,0:T(8,128)(2,1)S(1)} %copy-done.2, f32[8,128]{1,0:T(8,128)S(1)} %convert_element_type.5.mask, ...), custom_call_target="tpu_custom_call" | custom-call | flops 1610612736 | bytes 4194304 | tf_op jit(solution)/shard_map/saturate/pallas_call | solution.py:439
  49.6 0.2 collective-permute-done.8
  49.8 0.7 %collective-permute-start.9 = (bf16[8,80,256]{2,1,0:T(8,128)(2,1)S(1)}, bf16[8,80,256]{2,1,0:T(8,128)(2,1)S(1)}, u32[]{:S(2)}, u32[]{:S(2)}) collective-permute-start(bf16[8,80,256]{2,1,0:T(8,128)(2,1)S(1)} %pad_maximum_fusion.2), channel_id=1, source_target_pairs={{0,16},{4,20},{8,24},{12,28},{16,0},{20,4},{24,8},{28,12},{1,17},{... | collective-permute-start | bytes 983048 | tf_op jit(solution)/shard_map/ppermute | solution.py:340
  50.6 4.5 %saturate.7 = (bf16[8,48,256]{2,1,0:T(8,128)(2,1)S(1)}, f32[8,48,1]{2,1,0:T(8,128)S(1)}) custom-call(bf16[130,48,256]{2,1,0:T(8,128)(2,1)S(1)} %get-tuple-element.55.packed, bf16[256,160]{1,0:T(8,128)(2,1)S(1)} %maximum_maximum_fusion.weights, bf16[128,128]{1,0:T(8,128)(2,1)S(1)} %copy-done.2, f32[8,128]{1,0:T(8,128)S(1)} %convert_element_type.5.mask, ...), custom_call_target="tpu_custom_call" | custom-call | flops 1610612736 | bytes 4194304 | tf_op jit(solution)/shard_map/saturate/pallas_call | solution.py:439
  55.1 1.9 %collective-permute-done.9 = bf16[8,80,256]{2,1,0:T(8,128)(2,1)S(1)} collective-permute-done((bf16[8,80,256]{2,1,0:T(8,128)(2,1)S(1)}, bf16[8,80,256]{2,1,0:T(8,128)(2,1)S(1)}, u32[]{:S(2)}, u32[]{:S(2)}) %collective-permute-start.9) | collective-permute-done | bytes 327712 | tf_op jit(solution)/shard_map/ppermute | solution.py:340
  57.1 0.9 %moments.1 = (bf16[16,128,256]{2,1,0:T(8,128)(2,1)S(1)}, f32[16,128,1]{2,1,0:T(8,128)S(1)}) custom-call(bf16[16,128,256]{2,1,0:T(8,128)(2,1)S(1)} %bitcast.29), custom_call_target="tpu_custom_call" | custom-call | tf_op jit(solution)/shard_map/moments/pallas_call | solution.py:411
  58.0 1.2 %collective-permute-done.10 = bf16[16,80,256]{2,1,0:T(8,128)(2,1)S(1)} collective-permute-done((bf16[16,80,256]{2,1,0:T(8,128)(2,1)S(1)}, bf16[16,80,256]{2,1,0:T(8,128)(2,1)S(1)}, u32[]{:S(2)}, u32[]{:S(2)}) %collective-permute-start.10) | collective-permute-done | bytes 655392 | tf_op jit(solution)/shard_map/ppermute | solution.py:340
  59.2 0.1 pad_maximum_fusion.refs_0_
  59.3 9.9 %update.1 = bf16[24,128,256]{2,1,0:T(8,128)(2,1)} custom-call(bf16[32,80,256]{2,1,0:T(8,128)(2,1)S(1)} %pad_maximum_fusion.refs_0_, bf16[16,128,256]{2,1,0:T(8,128)(2,1)S(1)} %get-tuple-element.59.refs_1_, f32[16,128,1]{2,1,0:T(8,128)S(1)} %get-tuple-element.60.refs_2_, bf16[8,16,256]{2,1,0:T(8,128)(2,1)S(1)} %get-tuple-element.61.refs_3_, ...), custom_call_target="tpu_custom_call" | custom-call | tf_op jit(solution)/shard_map/update/pallas_call | solution.py:470
  (48 shorter events, 0.9 us)
Async XLA Ops:
  0.0 11.9 %copy-start = (bf16[54,32]{0,1:T(8,128)(2,1)S(1)}, bf16[54,32]{0,1:T(8,128)(2,1)}, u32[]{:S(2)}) copy-start(bf16[54,32]{0,1:T(8,128)(2,1)} %param.13) | copy-start | bytes 10372
  0.0 8.9 %copy-start.1 = (bf16[2,2,4,128,256]{4,3,2,1,0:T(8,128)(2,1)S(1)}, bf16[2,2,4,128,256]{4,3,2,1,0:T(8,128)(2,1)}, u32[]{:S(2)}) copy-start(bf16[2,2,4,128,256]{4,3,2,1,0:T(8,128)(2,1)} %param.11) | copy-start | bytes 3145732
  1.9 9.9 %copy-start.7 = (f32[32]{0:T(128)S(1)}, f32[32]{0:T(128)}, u32[]{:S(2)}) copy-start(f32[32]{0:T(128)} %param.14) | copy-start | bytes 388
  1.9 10.0 %copy-start.6 = (bf16[54,1152]{1,0:T(8,128)(2,1)S(1)}, bf16[54,1152]{1,0:T(8,128)(2,1)}, u32[]{:S(2)}) copy-start(bf16[54,1152]{1,0:T(8,128)(2,1)} %constant.12.clone) | copy-start | bytes 373252
  1.9 11.3 %collective-permute-start.3 = (bf16[2,2,1,128,256]{4,3,2,1,0:T(8,128)(2,1)S(1)}, bf16[2,2,1,128,256]{4,3,2,1,0:T(8,128)(2,1)S(1)}, u32[]{:S(2)}, u32[]{:S(2)}) collective-permute-start(bf16[2,2,1,128,256]{4,3,2,1,0:T(8,128)(2,1)S(1)} %get-tuple-element.69), channel_id=1, source_target_pairs={{1,0},{2,1},{3,2},{5,4},{6,5},{7,6},{9,8},{10,9},{11,10},{13,12},{... | collective-permute-start | bytes 786440 | tf_op jit(solution)/shard_map/ppermute | solution.py:331
  3.3 9.2 %copy-start.10 = (f32[32]{0:T(128)S(1)}, f32[32]{0:T(128)}, u32[]{:S(2)}) copy-start(f32[32]{0:T(128)} %param.15) | copy-start | bytes 388
  3.3 11.4 %collective-permute-start.2 = (bf16[2,2,1,128,256]{4,3,2,1,0:T(8,128)(2,1)}, bf16[2,2,1,128,256]{4,3,2,1,0:T(8,128)(2,1)S(1)}, u32[]{:S(2)}, u32[]{:S(2)}) collective-permute-start(bf16[2,2,1,128,256]{4,3,2,1,0:T(8,128)(2,1)} %get-tuple-element.70), channel_id=1, source_target_pairs={{0,1},{1,2},{2,3},{4,5},{5,6},{6,7},{8,9},{9,10},{10,11},{12,13},{... | collective-permute-start | bytes 786440 | tf_op jit(solution)/shard_map/ppermute | solution.py:331
  10.0 21.5 %collective-permute-start.1 = (bf16[2,1,4,128,256]{4,3,2,1,0:T(8,128)(2,1)}, bf16[2,1,4,128,256]{4,3,2,1,0:T(8,128)(2,1)S(1)}, u32[]{:S(2)}, u32[]{:S(2)}) collective-permute-start(bf16[2,1,4,128,256]{4,3,2,1,0:T(8,128)(2,1)} %get-tuple-element.71), channel_id=1, source_target_pairs={{4,0},{8,4},{12,8},{16,12},{20,16},{24,20},{28,24},{0,28},{5,1},{9... | collective-permute-start | bytes 1572872 | tf_op jit(solution)/shard_map/ppermute | solution.py:331
  11.7 19.7 %collective-permute-start = (bf16[2,1,4,128,256]{4,3,2,1,0:T(8,128)(2,1)}, bf16[2,1,4,128,256]{4,3,2,1,0:T(8,128)(2,1)S(1)}, u32[]{:S(2)}, u32[]{:S(2)}) collective-permute-start(bf16[2,1,4,128,256]{4,3,2,1,0:T(8,128)(2,1)} %get-tuple-element.72), channel_id=1, source_target_pairs={{0,4},{4,8},{8,12},{12,16},{16,20},{20,24},{24,28},{28,0},{1,5},{5... | collective-permute-start | bytes 1572872 | tf_op jit(solution)/shard_map/ppermute | solution.py:331
  12.0 6.9 %copy-start.8 = (f32[64]{0:T(128)S(1)}, f32[64]{0:T(128)}, u32[]{:S(2)}) copy-start(f32[64]{0:T(128)} %param.17) | copy-start | bytes 772
  12.1 6.8 %copy-start.9 = (f32[64]{0:T(128)S(1)}, f32[64]{0:T(128)}, u32[]{:S(2)}) copy-start(f32[64]{0:T(128)} %param.18) | copy-start | bytes 772
  12.4 7.4 %copy-start.4 = (s32[2,4,128]{2,1,0:T(4,128)S(1)}, s32[2,4,128]{2,1,0:T(4,128)}, u32[]{:S(2)}) copy-start(s32[2,4,128]{2,1,0:T(4,128)} %param.12) | copy-start | bytes 12292
  13.3 18.2 %copy-start.3 = (bf16[256,256]{1,0:T(8,128)(2,1)S(1)}, bf16[256,256]{1,0:T(8,128)(2,1)}, u32[]{:S(2)}) copy-start(bf16[256,256]{1,0:T(8,128)(2,1)} %constant.13.clone.swap_in) | copy-start | bytes 393220
  13.3 18.2 %copy-start.5 = (s32[64]{0:T(128)S(1)}, s32[64]{0:T(128)}, u32[]{:S(2)}) copy-start(s32[64]{0:T(128)} %cells.1) | copy-start | bytes 772
  15.5 15.9 %collective-permute-start.4 = (bf16[2,1,2,128,256]{4,3,2,1,0:T(8,128)(2,1)}, bf16[2,1,2,128,256]{4,3,2,1,0:T(8,128)(2,1)S(1)}, u32[]{:S(2)}, u32[]{:S(2)}) collective-permute-start(bf16[2,1,2,128,256]{4,3,2,1,0:T(8,128)(2,1)} %pad_maximum_fusion.3), channel_id=1, source_target_pairs={{0,4},{4,8},{8,12},{12,16},{16,20},{20,24},{24,28},{28,0},{1,5},{5... | collective-permute-start | bytes 786440 | tf_op jit(solution)/shard_map/ppermute | solution.py:331
  16.3 15.2 %collective-permute-start.5 = (bf16[2,1,2,128,256]{4,3,2,1,0:T(8,128)(2,1)}, bf16[2,1,2,128,256]{4,3,2,1,0:T(8,128)(2,1)S(1)}, u32[]{:S(2)}, u32[]{:S(2)}) collective-permute-start(bf16[2,1,2,128,256]{4,3,2,1,0:T(8,128)(2,1)} %pad_maximum_fusion.4), channel_id=1, source_target_pairs={{4,0},{8,4},{12,8},{16,12},{20,16},{24,20},{28,24},{0,28},{5,1},{9... | collective-permute-start | bytes 786440 | tf_op jit(solution)/shard_map/ppermute | solution.py:331
  31.5 6.1 %copy-start.2 = (bf16[128,128]{1,0:T(8,128)(2,1)S(1)}, bf16[128,128]{1,0:T(8,128)(2,1)}, u32[]{:S(2)}) copy-start(bf16[128,128]{1,0:T(8,128)(2,1)} %constant.14.clone.swap_out) | copy-start | bytes 98308
  34.9 5.0 %collective-permute-start.6 = (bf16[1,80,256]{2,1,0:T(8,128)(2,1)S(1)}, bf16[1,80,256]{2,1,0:T(8,128)(2,1)S(1)}, u32[]{:S(2)}, u32[]{:S(2)}) collective-permute-start(bf16[1,80,256]{2,1,0:T(8,128)(2,1)S(1)} %bitcast.36), channel_id=1, source_target_pairs={{0,2},{1,3},{2,0},{3,1},{4,6},{5,7},{6,4},{7,5},{8,10},{9,11},{10,... | collective-permute-start | bytes 122888 | tf_op jit(solution)/shard_map/ppermute | solution.py:340
  39.9 4.5 %collective-permute-start.7 = (bf16[2,80,256]{2,1,0:T(8,128)(2,1)S(1)}, bf16[2,80,256]{2,1,0:T(8,128)(2,1)S(1)}, u32[]{:S(2)}, u32[]{:S(2)}) collective-permute-start(bf16[2,80,256]{2,1,0:T(8,128)(2,1)S(1)} %pad_maximum_fusion.6), channel_id=1, source_target_pairs={{0,1},{1,0},{2,3},{3,2},{4,5},{5,4},{6,7},{7,6},{8,9},{9,8},{10,11... | collective-permute-start | bytes 245768 | tf_op jit(solution)/shard_map/ppermute | solution.py:340
  44.4 5.4 %collective-permute-start.8 = (bf16[4,80,256]{2,1,0:T(8,128)(2,1)S(1)}, bf16[4,80,256]{2,1,0:T(8,128)(2,1)S(1)}, u32[]{:S(2)}, u32[]{:S(2)}) collective-permute-start(bf16[4,80,256]{2,1,0:T(8,128)(2,1)S(1)} %pad_maximum_fusion.5), channel_id=1, source_target_pairs={{0,8},{4,12},{8,0},{12,4},{16,24},{20,28},{24,16},{28,20},{1,9},{5... | collective-permute-start | bytes 491528 | tf_op jit(solution)/shard_map/ppermute | solution.py:340
  49.8 7.1 %collective-permute-start.9 = (bf16[8,80,256]{2,1,0:T(8,128)(2,1)S(1)}, bf16[8,80,256]{2,1,0:T(8,128)(2,1)S(1)}, u32[]{:S(2)}, u32[]{:S(2)}) collective-permute-start(bf16[8,80,256]{2,1,0:T(8,128)(2,1)S(1)} %pad_maximum_fusion.2), channel_id=1, source_target_pairs={{0,16},{4,20},{8,24},{12,28},{16,0},{20,4},{24,8},{28,12},{1,17},{... | collective-permute-start | bytes 983048 | tf_op jit(solution)/shard_map/ppermute | solution.py:340
  57.0 2.2 %collective-permute-start.10 = (bf16[16,80,256]{2,1,0:T(8,128)(2,1)S(1)}, bf16[16,80,256]{2,1,0:T(8,128)(2,1)S(1)}, u32[]{:S(2)}, u32[]{:S(2)}) collective-permute-start(bf16[16,80,256]{2,1,0:T(8,128)(2,1)S(1)} %pad_maximum_fusion.1), channel_id=1, source_target_pairs={{0,4},{4,0},{8,12},{12,8},{16,20},{20,16},{24,28},{28,24},{1,5},{5... | collective-permute-start | bytes 1966088 | tf_op jit(solution)/shard_map/ppermute | solution.py:340

commit v3 on v1

--- a/solution.py
+++ b/solution.py
@@ -377,10 +377,12 @@
     rows = planes * columns
     observed = obs_cells.shape[0]
 
-    left = shift(fields[:, :, -1:], "face", 1, False)
-    right = shift(fields[:, :, :1], "face", -1, False)
-    low = shift(fields[:, -1:], "cores", 1, True)
-    high = shift(fields[:, :1], "cores", -1, True)
+    ends = (fields[:, :, -1:], fields[:, :, :1], fields[:, -1:], fields[:, :1])
+    left, right, low, high = lax.optimization_barrier(ends)
+    low = shift(low, "cores", 1, True)
+    high = shift(high, "cores", -1, True)
+    left = shift(left, "face", 1, False)
+    right = shift(right, "face", -1, False)
     low_sides = jnp.concatenate([left[:, -1:], right[:, -1:]], axis=2)
     high_sides = jnp.concatenate([left[:, :1], right[:, :1]], axis=2)
     corner_low = shift(low_sides, "cores", 1, True)

time: 69.5 us -> 70.9 us (1.020)
  starting transfers between devices: 17.1 us -> 20.4 us
  waiting for transfers between devices: 17.1 us -> 15.2 us
    ppermute x6, waiting for transfers between devices: 12.7 us -> 9.45 us  [shift(): return lax.ppermute(value, axis, pairs)]
    ppermute x5, starting transfers between devices: 5.68 us -> 8.8 us  [gather_rows(): other = lax.ppermute(block, axis, [(i, i ^ bit) for i in range(count)])]
    ppermute x5, waiting for transfers between devices: 4.45 us -> 5.78 us  [gather_rows(): other = lax.ppermute(block, axis, [(i, i ^ bit) for i in range(count)])]
  transfers between devices with their start and end apart: 11 -> 11, of which waited for: 8 -> 8; matrix products, arithmetic and copies ran while one was open for 8% -> 6% of each run, Pallas kernels for 20% -> 20%
where the time goes in v3:
time: 70.9 us; the launch traced here: 70.7 us
  Pallas kernels  27.3 us (39%)
  starting transfers between devices  20.4 us (29%)
  waiting for transfers between devices  15.2 us (21%)
  local copies, waits for them, and re-layouts  5.4 us (8%)
  other arithmetic  1.94 us (3%)
    pallas_call x4, Pallas kernels, saturate(): pl.pallas_call(functools.partial(saturate_kernel, starts[n]), out_shape=m...  13.1 us
    ppermute x6, starting transfers between devices, shift(): return lax.ppermute(value, axis, pairs)  11.6 us
    pallas_call x1, Pallas kernels, shards(): pl.pallas_call(functools.partial(update_kernel, gathered), out_shape=jax....  9.96 us
    ppermute x6, waiting for transfers between devices, shift(): return lax.ppermute(value, axis, pairs)  9.45 us
    ppermute x5, starting transfers between devices, gather_rows(): other = lax.ppermute(block, axis, [(i, i ^ bit) for i in range(count)])  8.8 us
    ppermute x5, waiting for transfers between devices, gather_rows(): other = lax.ppermute(block, axis, [(i, i ^ bit) for i in range(count)])  5.78 us
    pallas_call x1, Pallas kernels, shards(): pl.pallas_call(observe_kernel, out_shape=(jax.ShapeDtypeStruct((lanes + 2...  3.39 us
    slice x2, local copies, waits for them, and re-layouts, shards(): ends = (fields[:, :, -1:], fields[:, :, :1], fields[:, -1:], fields[:, :1])  2.93 us
  transfers between devices with their start and end apart: 11, of which 8 were waited for; matrix products, arithmetic and copies ran while one was open for 6% of the time, Pallas kernels for 20%

profile of v3, /device:TPU:0, one launch (start us, length us, event | category | flops | bytes accessed | tf_op | source)
XLA Modules:
  0.0 70.7 jit_solution(9081683916120086035)
XLA Ops:
  0.0 1.9 %fusion.6 = (bf16[2,2,1,128,256]{4,3,2,1,0:T(8,128)(2,1)}, bf16[2,2,1,128,256]{4,3,2,1,0:T(8,128)(2,1)S(1)}) fusion(bf16[2,2,4,128,256]{4,3,2,1,0:T(8,128)(2,1)} %param.11), kind=kLoop, calls=%fused_computation.24 | loop fusion | bytes 1048576 | tf_op jit(solution)/shard_map/slice | solution.py:380
  1.9 1.1 %fusion.5 = (bf16[2,1,4,128,256]{4,3,2,1,0:T(8,128)(2,1)}, bf16[2,1,4,128,256]{4,3,2,1,0:T(8,128)(2,1)}) fusion(bf16[2,2,4,128,256]{4,3,2,1,0:T(8,128)(2,1)S(1)} %copy-done.1), kind=kLoop, calls=%fused_computation.23 | loop fusion | bytes 2097152 | tf_op jit(solution)/shard_map/slice | solution.py:380
  2.9 4.9 %collective-permute-start.2 = (bf16[2,2,1,128,256]{4,3,2,1,0:T(8,128)(2,1)S(1)}, bf16[2,2,1,128,256]{4,3,2,1,0:T(8,128)(2,1)S(1)}, u32[]{:S(2)}, u32[]{:S(2)}) collective-permute-start(bf16[2,2,1,128,256]{4,3,2,1,0:T(8,128)(2,1)S(1)} %get-tuple-element.43), channel_id=1, source_target_pairs={{0,1},{1,2},{2,3},{4,5},{5,6},{6,7},{8,9},{9,10},{10,11},{12,13},{... | collective-permute-start | bytes 786440 | tf_op jit(solution)/shard_map/ppermute | solution.py:331
  7.9 1.3 %collective-permute-start.3 = (bf16[2,2,1,128,256]{4,3,2,1,0:T(8,128)(2,1)}, bf16[2,2,1,128,256]{4,3,2,1,0:T(8,128)(2,1)S(1)}, u32[]{:S(2)}, u32[]{:S(2)}) collective-permute-start(bf16[2,2,1,128,256]{4,3,2,1,0:T(8,128)(2,1)} %get-tuple-element.44), channel_id=1, source_target_pairs={{1,0},{2,1},{3,2},{5,4},{6,5},{7,6},{9,8},{10,9},{11,10},{13,12},{... | collective-permute-start | bytes 786440 | tf_op jit(solution)/shard_map/ppermute | solution.py:331
  9.3 2.6 %collective-permute-start.1 = (bf16[2,1,4,128,256]{4,3,2,1,0:T(8,128)(2,1)}, bf16[2,1,4,128,256]{4,3,2,1,0:T(8,128)(2,1)S(1)}, u32[]{:S(2)}, u32[]{:S(2)}) collective-permute-start(bf16[2,1,4,128,256]{4,3,2,1,0:T(8,128)(2,1)} %get-tuple-element.42), channel_id=1, source_target_pairs={{4,0},{8,4},{12,8},{16,12},{20,16},{24,20},{28,24},{0,28},{5,1},{9... | collective-permute-start | bytes 1572872 | tf_op jit(solution)/shard_map/ppermute | solution.py:331
  12.1 0.1 fusion.1
  12.2 0.2 mul.24
  12.6 0.8 %collective-permute-done.2 = bf16[2,2,1,128,256]{4,3,2,1,0:T(8,128)(2,1)S(1)} collective-permute-done((bf16[2,2,1,128,256]{4,3,2,1,0:T(8,128)(2,1)S(1)}, bf16[2,2,1,128,256]{4,3,2,1,0:T(8,128)(2,1)S(1)}, u32[]{:S(2)}, u32[]{:S(2)}) %collective-permute-start.2) | collective-permute-done | bytes 262176 | tf_op jit(solution)/shard_map/ppermute | solution.py:331
  13.5 4.3 %collective-permute-done.3 = bf16[2,2,1,128,256]{4,3,2,1,0:T(8,128)(2,1)S(1)} collective-permute-done((bf16[2,2,1,128,256]{4,3,2,1,0:T(8,128)(2,1)}, bf16[2,2,1,128,256]{4,3,2,1,0:T(8,128)(2,1)S(1)}, u32[]{:S(2)}, u32[]{:S(2)}) %collective-permute-start.3) | collective-permute-done | bytes 262176 | tf_op jit(solution)/shard_map/ppermute | solution.py:331
  17.8 0.7 %pad_maximum_fusion.3 = bf16[2,1,2,128,256]{4,3,2,1,0:T(8,128)(2,1)} fusion(bf16[2,1,1,128,256]{4,3,2,1,0:T(8,128)(2,1)S(1)} %get-tuple-element.84, bf16[2,1,1,128,256]{4,3,2,1,0:T(8,128)(2,1)S(1)} %get-tuple-element.82), kind=kLoop, calls=%fused_computation.6 | loop fusion | flops 131072 | bytes 524288 | tf_op jit(solution)/shard_map/concatenate | solution.py:386
  18.5 0.7 %pad_maximum_fusion.4 = bf16[2,1,2,128,256]{4,3,2,1,0:T(8,128)(2,1)} fusion(bf16[2,1,1,128,256]{4,3,2,1,0:T(8,128)(2,1)S(1)} %get-tuple-element.83, bf16[2,1,1,128,256]{4,3,2,1,0:T(8,128)(2,1)S(1)} %get-tuple-element.81), kind=kLoop, calls=%fused_computation.7 | loop fusion | flops 131072 | bytes 524288 | tf_op jit(solution)/shard_map/concatenate | solution.py:387
  19.3 2.6 %collective-permute-start.5 = (bf16[2,1,2,128,256]{4,3,2,1,0:T(8,128)(2,1)}, bf16[2,1,2,128,256]{4,3,2,1,0:T(8,128)(2,1)S(1)}, u32[]{:S(2)}, u32[]{:S(2)}) collective-permute-start(bf16[2,1,2,128,256]{4,3,2,1,0:T(8,128)(2,1)} %pad_maximum_fusion.4), channel_id=1, source_target_pairs={{4,0},{8,4},{12,8},{16,12},{20,16},{24,20},{28,24},{0,28},{5,1},{9... | collective-permute-start | bytes 786440 | tf_op jit(solution)/shard_map/ppermute | solution.py:331
  21.9 0.9 %mul.21 = bf16[32,8,144]{2,1,0:T(8,128)(2,1)} reshape(bf16[32,1152]{1,0:T(8,128)(2,1)S(1)} %fusion.1) | data formatting | bytes 147456 | tf_op jit(solution)/shard_map/mul | solution.py:401
  23.0 0.9 %copy.24 = bf16[32,8,144]{2,0,1:T(8,128)(2,1)S(1)} copy(bf16[32,8,144]{2,1,0:T(8,128)(2,1)} %mul.21) | data formatting | bytes 147456 | tf_op jit(solution)/shard_map/mul | solution.py:401
  24.0 4.3 %collective-permute-done.4 = bf16[2,1,2,128,256]{4,3,2,1,0:T(8,128)(2,1)S(1)} collective-permute-done((bf16[2,1,2,128,256]{4,3,2,1,0:T(8,128)(2,1)}, bf16[2,1,2,128,256]{4,3,2,1,0:T(8,128)(2,1)S(1)}, u32[]{:S(2)}, u32[]{:S(2)}) %collective-permute-start.4) | collective-permute-done | bytes 262176 | tf_op jit(solution)/shard_map/ppermute | solution.py:331
  28.3 0.1 collective-permute-done.5
  28.4 3.4 %observe.1 = (bf16[130,48,256]{2,1,0:T(8,128)(2,1)S(1)}, bf16[80,256]{1,0:T(8,128)(2,1)S(1)}) custom-call(bf16[16,128,256]{2,1,0:T(8,128)(2,1)S(1)} %bitcast.28, bf16[8,128,256]{2,1,0:T(8,128)(2,1)S(1)} %bitcast.32, bf16[8,128,256]{2,1,0:T(8,128)(2,1)S(1)} %bitcast.33, bf16[4,128,256]{2,1,0:T(8,128)(2,1)S(1)} %bitcast.30, bf16[4,128,256]{2,1,0:T(8,128)(2,1)S(1)} %bitcast.31, ...), custom_call_target="tpu_custom_call" | custom-call | tf_op jit(solution)/shard_map/observe/pallas_call | solution.py:423
  31.8 3.7 %collective-permute-start.6 = (bf16[1,80,256]{2,1,0:T(8,128)(2,1)S(1)}, bf16[1,80,256]{2,1,0:T(8,128)(2,1)S(1)}, u32[]{:S(2)}, u32[]{:S(2)}) collective-permute-start(bf16[1,80,256]{2,1,0:T(8,128)(2,1)S(1)} %bitcast.36), channel_id=1, source_target_pairs={{0,2},{1,3},{2,0},{3,1},{4,6},{5,7},{6,4},{7,5},{8,10},{9,11},{10,... | collective-permute-start | bytes 122888 | tf_op jit(solution)/shard_map/ppermute | solution.py:340
  35.5 2.0 %saturate.4 = (bf16[8,16,256]{2,1,0:T(8,128)(2,1)S(1)}, f32[8,16,1]{2,1,0:T(8,128)S(1)}) custom-call(bf16[130,48,256]{2,1,0:T(8,128)(2,1)S(1)} %get-tuple-element.63.packed, bf16[256,160]{1,0:T(8,128)(2,1)S(1)} %maximum_maximum_fusion.weights, bf16[128,128]{1,0:T(8,128)(2,1)S(1)} %copy-done.2, f32[8,128]{1,0:T(8,128)S(1)} %convert_element_type.5.mask, ...), custom_call_target="tpu_custom_call" | custom-call | flops 536870912 | bytes 4194304 | tf_op jit(solution)/shard_map/saturate/pallas_call | solution.py:441
  37.6 2.0 %collective-permute-start.7 = (bf16[2,80,256]{2,1,0:T(8,128)(2,1)S(1)}, bf16[2,80,256]{2,1,0:T(8,128)(2,1)S(1)}, u32[]{:S(2)}, u32[]{:S(2)}) collective-permute-start(bf16[2,80,256]{2,1,0:T(8,128)(2,1)S(1)} %pad_maximum_fusion.6), channel_id=1, source_target_pairs={{0,1},{1,0},{2,3},{3,2},{4,5},{5,4},{6,7},{7,6},{8,9},{9,8},{10,11... | collective-permute-start | bytes 245768 | tf_op jit(solution)/shard_map/ppermute | solution.py:340
  39.6 2.0 %saturate.5 = (bf16[8,16,256]{2,1,0:T(8,128)(2,1)S(1)}, f32[8,16,1]{2,1,0:T(8,128)S(1)}) custom-call(bf16[130,48,256]{2,1,0:T(8,128)(2,1)S(1)} %get-tuple-element.63.packed, bf16[256,160]{1,0:T(8,128)(2,1)S(1)} %maximum_maximum_fusion.weights, bf16[128,128]{1,0:T(8,128)(2,1)S(1)} %copy-done.2, f32[8,128]{1,0:T(8,128)S(1)} %convert_element_type.5.mask, ...), custom_call_target="tpu_custom_call" | custom-call | flops 536870912 | bytes 4194304 | tf_op jit(solution)/shard_map/saturate/pallas_call | solution.py:441
  41.6 1.1 %collective-permute-done.7 = bf16[2,80,256]{2,1,0:T(8,128)(2,1)S(1)} collective-permute-done((bf16[2,80,256]{2,1,0:T(8,128)(2,1)S(1)}, bf16[2,80,256]{2,1,0:T(8,128)(2,1)S(1)}, u32[]{:S(2)}, u32[]{:S(2)}) %collective-permute-start.7) | collective-permute-done | bytes 81952 | tf_op jit(solution)/shard_map/ppermute | solution.py:340
  42.7 1.6 %collective-permute-start.8 = (bf16[4,80,256]{2,1,0:T(8,128)(2,1)S(1)}, bf16[4,80,256]{2,1,0:T(8,128)(2,1)S(1)}, u32[]{:S(2)}, u32[]{:S(2)}) collective-permute-start(bf16[4,80,256]{2,1,0:T(8,128)(2,1)S(1)} %pad_maximum_fusion.5), channel_id=1, source_target_pairs={{0,8},{4,12},{8,0},{12,4},{16,24},{20,28},{24,16},{28,20},{1,9},{5... | collective-permute-start | bytes 491528 | tf_op jit(solution)/shard_map/ppermute | solution.py:340
  44.2 4.5 %saturate.6 = (bf16[8,48,256]{2,1,0:T(8,128)(2,1)S(1)}, f32[8,48,1]{2,1,0:T(8,128)S(1)}) custom-call(bf16[130,48,256]{2,1,0:T(8,128)(2,1)S(1)} %get-tuple-element.63.packed, bf16[256,160]{1,0:T(8,128)(2,1)S(1)} %maximum_maximum_fusion.weights, bf16[128,128]{1,0:T(8,128)(2,1)S(1)} %copy-done.2, f32[8,128]{1,0:T(8,128)S(1)} %convert_element_type.5.mask, ...), custom_call_target="tpu_custom_call" | custom-call | flops 1610612736 | bytes 4194304 | tf_op jit(solution)/shard_map/saturate/pallas_call | solution.py:441
  48.8 0.2 collective-permute-done.8
  49.0 1.5 %collective-permute-start.9 = (bf16[8,80,256]{2,1,0:T(8,128)(2,1)S(1)}, bf16[8,80,256]{2,1,0:T(8,128)(2,1)S(1)}, u32[]{:S(2)}, u32[]{:S(2)}) collective-permute-start(bf16[8,80,256]{2,1,0:T(8,128)(2,1)S(1)} %pad_maximum_fusion.2), channel_id=1, source_target_pairs={{0,16},{4,20},{8,24},{12,28},{16,0},{20,4},{24,8},{28,12},{1,17},{... | collective-permute-start | bytes 983048 | tf_op jit(solution)/shard_map/ppermute | solution.py:340
  50.5 4.5 %saturate.7 = (bf16[8,48,256]{2,1,0:T(8,128)(2,1)S(1)}, f32[8,48,1]{2,1,0:T(8,128)S(1)}) custom-call(bf16[130,48,256]{2,1,0:T(8,128)(2,1)S(1)} %get-tuple-element.63.packed, bf16[256,160]{1,0:T(8,128)(2,1)S(1)} %maximum_maximum_fusion.weights, bf16[128,128]{1,0:T(8,128)(2,1)S(1)} %copy-done.2, f32[8,128]{1,0:T(8,128)S(1)} %convert_element_type.5.mask, ...), custom_call_target="tpu_custom_call" | custom-call | flops 1610612736 | bytes 4194304 | tf_op jit(solution)/shard_map/saturate/pallas_call | solution.py:441
  55.0 3.3 %collective-permute-done.9 = bf16[8,80,256]{2,1,0:T(8,128)(2,1)S(1)} collective-permute-done((bf16[8,80,256]{2,1,0:T(8,128)(2,1)S(1)}, bf16[8,80,256]{2,1,0:T(8,128)(2,1)S(1)}, u32[]{:S(2)}, u32[]{:S(2)}) %collective-permute-start.9) | collective-permute-done | bytes 327712 | tf_op jit(solution)/shard_map/ppermute | solution.py:340
  58.5 0.9 %moments.1 = (bf16[16,128,256]{2,1,0:T(8,128)(2,1)S(1)}, f32[16,128,1]{2,1,0:T(8,128)S(1)}) custom-call(bf16[16,128,256]{2,1,0:T(8,128)(2,1)S(1)} %bitcast.29), custom_call_target="tpu_custom_call" | custom-call | tf_op jit(solution)/shard_map/moments/pallas_call | solution.py:413
  59.4 1.2 %collective-permute-done.10 = bf16[16,80,256]{2,1,0:T(8,128)(2,1)S(1)} collective-permute-done((bf16[16,80,256]{2,1,0:T(8,128)(2,1)S(1)}, bf16[16,80,256]{2,1,0:T(8,128)(2,1)S(1)}, u32[]{:S(2)}, u32[]{:S(2)}) %collective-permute-start.10) | collective-permute-done | bytes 655392 | tf_op jit(solution)/shard_map/ppermute | solution.py:340
  60.6 0.1 pad_maximum_fusion.refs_0_
  60.7 10.0 %update.1 = bf16[24,128,256]{2,1,0:T(8,128)(2,1)} custom-call(bf16[32,80,256]{2,1,0:T(8,128)(2,1)S(1)} %pad_maximum_fusion.refs_0_, bf16[16,128,256]{2,1,0:T(8,128)(2,1)S(1)} %get-tuple-element.67.refs_1_, f32[16,128,1]{2,1,0:T(8,128)S(1)} %get-tuple-element.68.refs_2_, bf16[8,16,256]{2,1,0:T(8,128)(2,1)S(1)} %get-tuple-element.69.refs_3_, ...), custom_call_target="tpu_custom_call" | custom-call | tf_op jit(solution)/shard_map/update/pallas_call | solution.py:472
  (48 shorter events, 1.0 us)
Async XLA Ops:
  0.0 12.0 %copy-start = (bf16[54,32]{0,1:T(8,128)(2,1)S(1)}, bf16[54,32]{0,1:T(8,128)(2,1)}, u32[]{:S(2)}) copy-start(bf16[54,32]{0,1:T(8,128)(2,1)} %param.13) | copy-start | bytes 10372
  0.0 1.9 %copy-start.1 = (bf16[2,2,4,128,256]{4,3,2,1,0:T(8,128)(2,1)S(1)}, bf16[2,2,4,128,256]{4,3,2,1,0:T(8,128)(2,1)}, u32[]{:S(2)}) copy-start(bf16[2,2,4,128,256]{4,3,2,1,0:T(8,128)(2,1)} %param.11) | copy-start | bytes 3145732
  1.9 10.0 %copy-start.7 = (f32[32]{0:T(128)S(1)}, f32[32]{0:T(128)}, u32[]{:S(2)}) copy-start(f32[32]{0:T(128)} %param.14) | copy-start | bytes 388
  1.9 10.2 %copy-start.6 = (bf16[54,1152]{1,0:T(8,128)(2,1)S(1)}, bf16[54,1152]{1,0:T(8,128)(2,1)}, u32[]{:S(2)}) copy-start(bf16[54,1152]{1,0:T(8,128)(2,1)} %constant.12.clone) | copy-start | bytes 373252
  1.9 10.7 %copy-start.10 = (f32[32]{0:T(128)S(1)}, f32[32]{0:T(128)}, u32[]{:S(2)}) copy-start(f32[32]{0:T(128)} %param.15) | copy-start | bytes 388
  2.9 10.5 %collective-permute-start.2 = (bf16[2,2,1,128,256]{4,3,2,1,0:T(8,128)(2,1)S(1)}, bf16[2,2,1,128,256]{4,3,2,1,0:T(8,128)(2,1)S(1)}, u32[]{:S(2)}, u32[]{:S(2)}) collective-permute-start(bf16[2,2,1,128,256]{4,3,2,1,0:T(8,128)(2,1)S(1)} %get-tuple-element.43), channel_id=1, source_target_pairs={{0,1},{1,2},{2,3},{4,5},{5,6},{6,7},{8,9},{9,10},{10,11},{12,13},{... | collective-permute-start | bytes 786440 | tf_op jit(solution)/shard_map/ppermute | solution.py:331
  7.9 9.9 %collective-permute-start.3 = (bf16[2,2,1,128,256]{4,3,2,1,0:T(8,128)(2,1)}, bf16[2,2,1,128,256]{4,3,2,1,0:T(8,128)(2,1)S(1)}, u32[]{:S(2)}, u32[]{:S(2)}) collective-permute-start(bf16[2,2,1,128,256]{4,3,2,1,0:T(8,128)(2,1)} %get-tuple-element.44), channel_id=1, source_target_pairs={{1,0},{2,1},{3,2},{5,4},{6,5},{7,6},{9,8},{10,9},{11,10},{13,12},{... | collective-permute-start | bytes 786440 | tf_op jit(solution)/shard_map/ppermute | solution.py:331
  9.2 19.2 %collective-permute-start = (bf16[2,1,4,128,256]{4,3,2,1,0:T(8,128)(2,1)}, bf16[2,1,4,128,256]{4,3,2,1,0:T(8,128)(2,1)S(1)}, u32[]{:S(2)}, u32[]{:S(2)}) collective-permute-start(bf16[2,1,4,128,256]{4,3,2,1,0:T(8,128)(2,1)} %get-tuple-element.41), channel_id=1, source_target_pairs={{0,4},{4,8},{8,12},{12,16},{16,20},{20,24},{24,28},{28,0},{1,5},{5... | collective-permute-start | bytes 1572872 | tf_op jit(solution)/shard_map/ppermute | solution.py:331
  9.3 19.2 %collective-permute-start.1 = (bf16[2,1,4,128,256]{4,3,2,1,0:T(8,128)(2,1)}, bf16[2,1,4,128,256]{4,3,2,1,0:T(8,128)(2,1)S(1)}, u32[]{:S(2)}, u32[]{:S(2)}) collective-permute-start(bf16[2,1,4,128,256]{4,3,2,1,0:T(8,128)(2,1)} %get-tuple-element.42), channel_id=1, source_target_pairs={{4,0},{8,4},{12,8},{16,12},{20,16},{24,20},{28,24},{0,28},{5,1},{9... | collective-permute-start | bytes 1572872 | tf_op jit(solution)/shard_map/ppermute | solution.py:331
  12.2 9.7 %copy-start.8 = (f32[64]{0:T(128)S(1)}, f32[64]{0:T(128)}, u32[]{:S(2)}) copy-start(f32[64]{0:T(128)} %param.17) | copy-start | bytes 772
  12.2 9.7 %copy-start.9 = (f32[64]{0:T(128)S(1)}, f32[64]{0:T(128)}, u32[]{:S(2)}) copy-start(f32[64]{0:T(128)} %param.18) | copy-start | bytes 772
  12.5 10.3 %copy-start.4 = (s32[2,4,128]{2,1,0:T(4,128)S(1)}, s32[2,4,128]{2,1,0:T(4,128)}, u32[]{:S(2)}) copy-start(s32[2,4,128]{2,1,0:T(4,128)} %param.12) | copy-start | bytes 12292
  13.4 15.0 %copy-start.3 = (bf16[256,256]{1,0:T(8,128)(2,1)S(1)}, bf16[256,256]{1,0:T(8,128)(2,1)}, u32[]{:S(2)}) copy-start(bf16[256,256]{1,0:T(8,128)(2,1)} %constant.13.clone.swap_in) | copy-start | bytes 393220
  13.5 15.0 %copy-start.5 = (s32[64]{0:T(128)S(1)}, s32[64]{0:T(128)}, u32[]{:S(2)}) copy-start(s32[64]{0:T(128)} %cells.1) | copy-start | bytes 772
  18.5 9.8 %collective-permute-start.4 = (bf16[2,1,2,128,256]{4,3,2,1,0:T(8,128)(2,1)}, bf16[2,1,2,128,256]{4,3,2,1,0:T(8,128)(2,1)S(1)}, u32[]{:S(2)}, u32[]{:S(2)}) collective-permute-start(bf16[2,1,2,128,256]{4,3,2,1,0:T(8,128)(2,1)} %pad_maximum_fusion.3), channel_id=1, source_target_pairs={{0,4},{4,8},{8,12},{12,16},{16,20},{20,24},{24,28},{28,0},{1,5},{5... | collective-permute-start | bytes 786440 | tf_op jit(solution)/shard_map/ppermute | solution.py:331
  19.3 9.1 %collective-permute-start.5 = (bf16[2,1,2,128,256]{4,3,2,1,0:T(8,128)(2,1)}, bf16[2,1,2,128,256]{4,3,2,1,0:T(8,128)(2,1)S(1)}, u32[]{:S(2)}, u32[]{:S(2)}) collective-permute-start(bf16[2,1,2,128,256]{4,3,2,1,0:T(8,128)(2,1)} %pad_maximum_fusion.4), channel_id=1, source_target_pairs={{4,0},{8,4},{12,8},{16,12},{20,16},{24,20},{28,24},{0,28},{5,1},{9... | collective-permute-start | bytes 786440 | tf_op jit(solution)/shard_map/ppermute | solution.py:331
  28.4 7.1 %copy-start.2 = (bf16[128,128]{1,0:T(8,128)(2,1)S(1)}, bf16[128,128]{1,0:T(8,128)(2,1)}, u32[]{:S(2)}) copy-start(bf16[128,128]{1,0:T(8,128)(2,1)} %constant.14.clone.swap_out) | copy-start | bytes 98308
  31.8 5.7 %collective-permute-start.6 = (bf16[1,80,256]{2,1,0:T(8,128)(2,1)S(1)}, bf16[1,80,256]{2,1,0:T(8,128)(2,1)S(1)}, u32[]{:S(2)}, u32[]{:S(2)}) collective-permute-start(bf16[1,80,256]{2,1,0:T(8,128)(2,1)S(1)} %bitcast.36), channel_id=1, source_target_pairs={{0,2},{1,3},{2,0},{3,1},{4,6},{5,7},{6,4},{7,5},{8,10},{9,11},{10,... | collective-permute-start | bytes 122888 | tf_op jit(solution)/shard_map/ppermute | solution.py:340
  37.6 5.1 %collective-permute-start.7 = (bf16[2,80,256]{2,1,0:T(8,128)(2,1)S(1)}, bf16[2,80,256]{2,1,0:T(8,128)(2,1)S(1)}, u32[]{:S(2)}, u32[]{:S(2)}) collective-permute-start(bf16[2,80,256]{2,1,0:T(8,128)(2,1)S(1)} %pad_maximum_fusion.6), channel_id=1, source_target_pairs={{0,1},{1,0},{2,3},{3,2},{4,5},{5,4},{6,7},{7,6},{8,9},{9,8},{10,11... | collective-permute-start | bytes 245768 | tf_op jit(solution)/shard_map/ppermute | solution.py:340
  42.7 6.3 %collective-permute-start.8 = (bf16[4,80,256]{2,1,0:T(8,128)(2,1)S(1)}, bf16[4,80,256]{2,1,0:T(8,128)(2,1)S(1)}, u32[]{:S(2)}, u32[]{:S(2)}) collective-permute-start(bf16[4,80,256]{2,1,0:T(8,128)(2,1)S(1)} %pad_maximum_fusion.5), channel_id=1, source_target_pairs={{0,8},{4,12},{8,0},{12,4},{16,24},{20,28},{24,16},{28,20},{1,9},{5... | collective-permute-start | bytes 491528 | tf_op jit(solution)/shard_map/ppermute | solution.py:340
  49.0 9.3 %collective-permute-start.9 = (bf16[8,80,256]{2,1,0:T(8,128)(2,1)S(1)}, bf16[8,80,256]{2,1,0:T(8,128)(2,1)S(1)}, u32[]{:S(2)}, u32[]{:S(2)}) collective-permute-start(bf16[8,80,256]{2,1,0:T(8,128)(2,1)S(1)} %pad_maximum_fusion.2), channel_id=1, source_target_pairs={{0,16},{4,20},{8,24},{12,28},{16,0},{20,4},{24,8},{28,12},{1,17},{... | collective-permute-start | bytes 983048 | tf_op jit(solution)/shard_map/ppermute | solution.py:340
  58.4 2.2 %collective-permute-start.10 = (bf16[16,80,256]{2,1,0:T(8,128)(2,1)S(1)}, bf16[16,80,256]{2,1,0:T(8,128)(2,1)S(1)}, u32[]{:S(2)}, u32[]{:S(2)}) collective-permute-start(bf16[16,80,256]{2,1,0:T(8,128)(2,1)S(1)} %pad_maximum_fusion.1), channel_id=1, source_target_pairs={{0,4},{4,0},{8,12},{12,8},{16,20},{20,16},{24,28},{28,24},{1,5},{5... | collective-permute-start | bytes 1966088 | tf_op jit(solution)/shard_map/ppermute | solution.py:340
